TPU v7x, 128 devices: a whole 4x4x4 slice. The times are simulated.
128 devices in a mesh: sample: 32 (over z_hi, y, x), prompt: 2 (over z_lo), tensor: 2 (over core).
Axes of the slice: x: 4, y: 4, z: 4 (z_hi: 2, z_lo: 2; z = z_hi * 2 + z_lo), core: 2. Of those that a mesh axis runs over, the one named last changes fastest.
Arguments:
- hidden_input: bfloat16 [4, 96, 8192], P(None, 'prompt'), parts along dimension 1, may hold values from -6 to 6
- prompt_lengths: int32 [6], P('prompt'), parts along dimension 0, may hold values from 1 to 1024, 1920 in all
- prompt_states: float32 [6, 256, 64, 256], P('prompt', None, None, ('sample', 'tensor')), parts along dimension 0, may hold values from -0.8 to 0.8
- prompt_cache: bfloat16 [6, 1024, 8, 256], P('prompt', ('sample', 'tensor')), parts along dimension 0, may hold values from -6 to 6
- input_gain: float32 [8192], replicated, may hold values from 0.25 to 1.75
- gate_weight: bfloat16 [8192, 16384], P(None, ('sample', 'tensor')), may hold values from -0.0625 to 0.0625
- input_weight: bfloat16 [8192, 16384], P(None, ('sample', 'tensor')), may hold values from -0.0625 to 0.0625
- rate_weight: bfloat16 [8192, 256], P(None, ('sample', 'tensor')), may hold values from -0.0625 to 0.0625
- rate_bias: float32 [256], P(('sample', 'tensor')), may hold values from -3 to 1
- decay_log: float32 [256], P(('sample', 'tensor')), may hold values from -2 to 2
- skip_gain: float32 [256], P(('sample', 'tensor')), may hold values from 0.5 to 2
- state_io_weight: bfloat16 [8192, 4096], P(('sample', 'tensor')), may hold values from -0.0625 to 0.0625
- mix_gain: float32 [16384], P(('sample', 'tensor')), may hold values from 0.25 to 1.75
- mix_weight: bfloat16 [16384, 8192], P(('sample', 'tensor')), may hold values from -0.046875 to 0.046875
- middle_gain: float32 [8192], replicated, may hold values from 0.25 to 1.75
- query_weight: bfloat16 [8192, 8192], P(None, ('sample', 'tensor')), may hold values from -0.0625 to 0.0625
- key_value_weight: bfloat16 [8192, 2048], P(('sample', 'tensor')), may hold values from -0.0625 to 0.0625
- output_weight: bfloat16 [8192, 8192], P(('sample', 'tensor')), may hold values from -0.0625 to 0.0625
Outputs:
- layer_out: bfloat16 [384, 8192], P(('prompt', 'sample', 'tensor')), parts along dimension 0
There are 2 independent parts, one for each index of `prompt`. A program takes and returns all parts, laid end to end along the dimension named above; an argument that names none is the same for every part. Nothing has to cross between parts.
Inputs may be any that keep to these rules, and one draw needn't show every extreme that they name: `prompt_lengths`: every prompt has at least one valid position; the longest prompt fills all 1024 positions.
All inputs are finite; a program needn't handle non-finite values.
Results may differ from a plain program's by a relative error of at most 0.009.
The roundings to bfloat16 on the way count: a program that leaves them out, or rounds other values in their place, can miss the bound.
Values may be sent and summed in bfloat16 or wider, within the bound.
A program may use at most 128 MiB of HBM per device.

v0:
```python
import jax
import jax.numpy as jnp
from jax import lax
from jax.sharding import PartitionSpec as P

KVH = 8


def normalize(values, gain_row):
    scale = lax.rsqrt(jnp.mean(values * values, axis=-1, keepdims=True) + 1e-05)
    return values * scale * gain_row


def shards(
    hidden_input,
    prompt_lengths,
    prompt_states,
    prompt_cache,
    input_gain,
    gate_weight,
    input_weight,
    rate_weight,
    rate_bias,
    decay_log,
    skip_gain,
    state_io_weight,
    mix_gain,
    mix_weight,
    middle_gain,
    query_weight,
    key_value_weight,
    output_weight,
):
    joined = lax.axis_size(("sample", "tensor"))
    device_index = lax.axis_index(("sample", "tensor"))
    step_count, row_count, model_width = hidden_input.shape
    token_count = step_count * row_count
    prompt_count = prompt_lengths.shape[0]
    sample_count = row_count // prompt_count
    head_count = rate_weight.shape[1]
    head_dim = gate_weight.shape[1] // head_count
    state_size = prompt_states.shape[3] * joined
    group_count = state_io_weight.shape[1] // (2 * state_size)
    head_width = query_weight.shape[1]
    cache_length = prompt_cache.shape[1] * joined
    own_rows = token_count // joined
    start_row = device_index * own_rows
    feature_share = state_io_weight.shape[0]
    feature_start = device_index * feature_share
    flat_rows = hidden_input.reshape(token_count, model_width).astype(jnp.float32)
    normed = normalize(flat_rows, input_gain).astype(jnp.bfloat16)
    gate_proj = jnp.dot(normed, gate_weight, preferred_element_type=jnp.float32)
    inner_proj = jnp.dot(normed, input_weight, preferred_element_type=jnp.float32)
    rate_raw = jnp.dot(normed, rate_weight, preferred_element_type=jnp.float32)
    normed_share = lax.dynamic_slice_in_dim(normed, feature_start, feature_share, 1)
    io_term = jnp.dot(normed_share, state_io_weight, preferred_element_type=jnp.float32)
    io_all = lax.psum(io_term, ("sample", "tensor")).astype(jnp.bfloat16)
    group_index = device_index * group_count // joined
    io_own = lax.dynamic_slice_in_dim(
        io_all, group_index * 2 * state_size, 2 * state_size, 1
    ).astype(jnp.float32)
    start_state = lax.all_to_all(
        prompt_states.astype(jnp.bfloat16),
        ("sample", "tensor"),
        split_axis=1,
        concat_axis=3,
        tiled=True,
    ).astype(prompt_states.dtype)
    step_rate = jax.nn.softplus(rate_raw + rate_bias).reshape(step_count, row_count, head_count)
    decay_rate = jnp.exp(step_rate * -jnp.exp(decay_log))
    inner_heads = inner_proj.reshape(step_count, row_count, head_count, head_dim)
    io_steps = io_own.reshape(step_count, row_count, 2 * state_size)
    carried = jnp.repeat(start_state, sample_count, axis=0)
    results = []
    for moment in range(step_count):
        entering = step_rate[moment][:, :, None] * inner_heads[moment]
        carried = (
            decay_rate[moment][:, :, None, None] * carried
            + entering[:, :, :, None] * io_steps[moment][:, None, None, :state_size]
        )
        readout = jnp.einsum(
            "rhdn,rn->rhd",
            carried,
            io_steps[moment][:, state_size:],
            precision=lax.Precision.HIGHEST,
        )
        results.append(readout + skip_gain[None, :, None] * inner_heads[moment])
    mixed_out = jnp.stack(results).reshape(token_count, head_count * head_dim)
    gated_out = mixed_out * jax.nn.silu(gate_proj)
    square_sum = jnp.sum(gated_out * gated_out, axis=1)
    group_pick = (jnp.arange(group_count)[None, :] == group_index).astype(jnp.float32)
    group_totals = lax.psum(group_pick * square_sum[:, None], ("sample", "tensor"))
    group_width = head_count * head_dim * joined // group_count
    own_total = jnp.sum(group_totals * group_pick, axis=1)
    scaled = (gated_out * lax.rsqrt(own_total / group_width + 1e-05)[:, None] * mix_gain).astype(
        jnp.bfloat16
    )
    mix_full = lax.psum(
        jnp.dot(scaled, mix_weight, preferred_element_type=jnp.float32), ("sample", "tensor")
    )
    residual = flat_rows + mix_full
    middle = normalize(residual, middle_gain).astype(jnp.bfloat16)
    residual_own = lax.dynamic_slice_in_dim(residual, start_row, own_rows, 0)
    query_rows = (
        jnp.dot(middle, query_weight, preferred_element_type=jnp.float32) * head_width ** (-0.5)
    ).astype(jnp.bfloat16)
    middle_share = lax.dynamic_slice_in_dim(middle, feature_start, feature_share, 1)
    pair_term = jnp.dot(middle_share, key_value_weight, preferred_element_type=jnp.float32)
    pair_all = lax.psum(pair_term, ("sample", "tensor")).astype(jnp.bfloat16)
    pair_index = device_index * KVH // joined
    pair_own = lax.dynamic_slice_in_dim(pair_all, pair_index * 2 * head_width, 2 * head_width, 1)
    new_keys = pair_own[:, :head_width].reshape(step_count, row_count, head_width)
    new_values = pair_own[:, head_width:].reshape(step_count, row_count, head_width)
    spread = jnp.repeat(prompt_cache, joined // KVH, axis=2)
    cache_full = lax.all_to_all(
        spread, ("sample", "tensor"), split_axis=2, concat_axis=1, tiled=True
    )
    cache_keys = cache_full[:, :, 0, :head_width]
    cache_values = cache_full[:, :, 0, head_width:]
    query_grid = query_rows.reshape(step_count, prompt_count, sample_count, head_width)
    far_scores = jnp.einsum(
        "tpsd,pld->tpsl", query_grid, cache_keys, preferred_element_type=jnp.float32
    )
    valid_mask = jnp.arange(cache_length)[None, :] < prompt_lengths[:, None]
    far_scores = jnp.where(valid_mask[None, :, None, :], far_scores, -1e30).reshape(
        step_count, row_count, cache_length
    )
    query_steps = query_rows.reshape(step_count, row_count, head_width)
    near_scores = jnp.einsum(
        "trd,urd->tru", query_steps, new_keys, preferred_element_type=jnp.float32
    )
    causal = jnp.arange(step_count)[:, None] >= jnp.arange(step_count)[None, :]
    near_scores = jnp.where(causal[:, None, :], near_scores, -1e30)
    row_top = jnp.maximum(jnp.max(far_scores, axis=-1), jnp.max(near_scores, axis=-1))
    far_exp = jnp.exp(far_scores - row_top[..., None])
    near_exp = jnp.exp(near_scores - row_top[..., None])
    row_total = jnp.sum(far_exp, axis=-1) + jnp.sum(near_exp, axis=-1)
    far_weight = (far_exp / row_total[..., None]).astype(jnp.bfloat16)
    near_weight = (near_exp / row_total[..., None]).astype(jnp.bfloat16)
    far_part = jnp.einsum(
        "tpsl,pld->tpsd",
        far_weight.reshape(step_count, prompt_count, sample_count, cache_length),
        cache_values,
        preferred_element_type=jnp.float32,
    )
    near_part = jnp.einsum(
        "tru,urd->trd", near_weight, new_values, preferred_element_type=jnp.float32
    )
    attended = (
        (far_part.reshape(step_count, row_count, head_width) + near_part)
        .astype(jnp.bfloat16)
        .reshape(token_count, head_width)
    )
    attention_own = lax.psum_scatter(
        jnp.dot(attended, output_weight, preferred_element_type=jnp.float32),
        ("sample", "tensor"),
        scatter_dimension=0,
        tiled=True,
    )
    return (residual_own + attention_own).astype(jnp.bfloat16)


def solution(mesh):
    in_specs = (
        P(None, "prompt", None),
        P("prompt"),
        P("prompt", None, None, ("sample", "tensor")),
        P("prompt", ("sample", "tensor"), None, None),
        P(),
        P(None, ("sample", "tensor")),
        P(None, ("sample", "tensor")),
        P(None, ("sample", "tensor")),
        P(("sample", "tensor")),
        P(("sample", "tensor")),
        P(("sample", "tensor")),
        P(("sample", "tensor"), None),
        P(("sample", "tensor")),
        P(("sample", "tensor"), None),
        P(),
        P(None, ("sample", "tensor")),
        P(("sample", "tensor"), None),
        P(("sample", "tensor"), None),
    )
    out_specs = P(("prompt", "sample", "tensor"), None)
    return jax.shard_map(shards, mesh=mesh, in_specs=in_specs, out_specs=out_specs, check_vma=False)
```

profile of v0, /device:TPU:1, one launch (start us, length us, event | category | flops | bytes accessed | tf_op | source)
XLA Modules:
  0.0 2312.6 jit_solution(12397213504820725662)
XLA Ops:
  6.5 1.4 copy.190
  8.5 1.3 reshape.228
  9.8 12.3 all-to-all-start
  22.2 2.6 fusion.7
  24.9 2.7 fusion.9
  27.7 1.6 copy-done.2
  29.3 0.9 compare_select_fusion
  30.4 3.5 fusion.51
  33.9 355.8 %all-reduce.9 = bf16[192,4096]{1,0:T(8,128)(2,1)} all-reduce(f32[192,4096]{1,0:T(8,128)} %fusion.51), channel_id=1, replica_groups=mesh['sample'=32,'prompt'=2,'tensor'=2] {'sample','tensor'}, use_global_device_ids=true, to_apply=%region_1.0 | all-reduce | flops 786432 | bytes 4718592 | tf_op jit(solution)/shard_map/psum | solution.py:57
  389.7 0.9 dynamic-slice_convert_fusion
  390.7 0.7 fusion.58
  391.4 0.6 slice_bitcast_fusion.7
  392.0 4.1 fusion.63
  396.6 0.7 broadcast_multiply_fusion.3
  397.4 0.8 broadcast_multiply_fusion
  398.2 0.7 copy.117
  399.3 0.7 copy.124
  400.0 0.7 copy.126
  400.7 0.7 copy.128
  401.4 0.8 broadcast_multiply_fusion.1
  403.0 2.2 copy.121
  405.2 1.9 copy.122
  407.1 2.2 fusion
  409.3 7.4 fusion.41
  416.8 7.8 fusion.5
  424.7 10.4 fusion.6
  435.1 12.6 fusion.1
  448.3 4.2 multiply_reduce_fusion.1
  452.6 172.2 %psum.29 = f32[192,8]{0,1:T(8,128)S(1)} all-reduce(f32[192,8]{0,1:T(8,128)S(1)} %broadcast_multiply_fusion.4), channel_id=1, replica_groups=mesh['sample'=32,'prompt'=2,'tensor'=2] {'sample','tensor'}, use_global_device_ids=true, to_apply=%region_3.4 | all-reduce | flops 1536 | bytes 12288 | tf_op jit(solution)/shard_map/psum | solution.py:92
  624.9 5.9 fusion.34
  630.9 1.3 broadcast_in_dim.22
  632.2 5.6 all-to-all-start.1
  637.9 26.0 %all-to-all-done.1 = bf16[3,16,64,256]{3,1,0,2:T(8,128)(2,1)} async-done(((bf16[3,16,64,256]{3,1,0,2:T(8,128)(2,1)}), bf16[3,16,64,256]{3,1,0,2:T(8,128)(2,1)}, u32[]{:S(2)}, u32[]{:S(2)}) %all-to-all-start.1) | async-done | bytes 1572896 | tf_op jit(solution)/shard_map/all_to_all | solution.py:115
  663.9 2.8 copy.131
  666.7 620.1 %all-reduce.6.cloned.1.call-done = f32[192,8192]{1,0:T(8,128)} async-done(((f32[192,8192]{1,0:T(8,128)}), f32[192,8192]{1,0:T(8,128)}) %all-reduce.6.cloned.1.call-update) | async-done | bytes 6291472 | tf_op jit(solution)/shard_map/psum | solution.py:98
  1286.8 4.3 bitcast_add_fusion
  1291.9 0.8 multiply_convert_fusion
  1292.7 1.0 copy-done.1
  1293.7 1.7 copy-done.3
  1295.5 1.5 fusion.49
  1297.0 338.4 %all-reduce.10 = bf16[192,2048]{1,0:T(8,128)(2,1)S(1)} all-reduce(f32[192,2048]{1,0:T(8,128)} %fusion.49), channel_id=1, replica_groups=mesh['sample'=32,'prompt'=2,'tensor'=2] {'sample','tensor'}, use_global_device_ids=true, to_apply=%region_8.9 | all-reduce | flops 393216 | bytes 2359296 | tf_op jit(solution)/shard_map/psum | solution.py:109
  1635.5 3.5 fusion.29
  1639.4 1.6 fusion.62
  1642.3 1.5 convolution_bitcast_fusion
  1644.0 3.6 fusion.64
  1647.6 0.6 dynamic-slice
  1648.9 655.0 %all-reduce.8.cloned.1.call-done = f32[192,8192]{1,0:T(8,128)} async-done(((f32[192,8192]{1,0:T(8,128)}), f32[192,8192]{1,0:T(8,128)}) %all-reduce.8.cloned.1.call-update) | async-done | bytes 6291472
  2303.9 1.9 fusion.33
  (124 shorter events, 6.2 us)
Async XLA Ops:
  6.5 1637.5 %copy-start = (bf16[128,8192]{1,0:T(8,128)(2,1)S(1)}, bf16[128,8192]{1,0:T(8,128)(2,1)}, u32[]{:S(2)}) copy-start(bf16[128,8192]{1,0:T(8,128)(2,1)} %param.35) | copy-start | bytes 6291460
  6.5 18.4 copy-start.19
  7.9 21.3 copy-start.15
  8.0 21.3 copy-start.30
  9.8 392.4 %all-to-all-start = ((bf16[64,2,1536]{2,1,0:T(2,128)(2,1)}), bf16[64,2,1536]{2,1,0:T(2,128)(2,1)S(1)}, u32[]{:S(2)}, u32[]{:S(2)}) async-start(bf16[64,2,1536]{2,1,0:T(2,128)(2,1)} %reshape.228), calls=%async_computation | async-start | bytes 786432 | tf_op jit(solution)/shard_map/all_to_all | solution.py:62
  22.1 1264.6 %all-reduce.6.cloned.1.call-start = ((), (), s32[]{:S(2)}) async-start(), calls=%async_computation.2 | async-start | bytes 12582912 | tf_op jit(solution)/shard_map/psum | solution.py:98
  27.7 1.6 copy-start.2
  392.0 4.4 copy-start.31
  399.0 3.3 copy-start.4
  399.1 3.2 copy-start.6
  402.7 4.3 copy-start.9
  402.7 4.3 copy-start.14
  409.3 7.5 copy-start.13
  409.3 7.5 copy-start.16
  409.3 7.5 copy-start.23
  409.3 7.5 copy-start.24
  416.8 7.8 copy-start.12
  416.8 7.8 copy-start.17
  416.8 7.8 copy-start.22
  416.8 7.8 copy-start.25
  424.6 10.4 copy-start.11
  424.6 10.4 copy-start.18
  424.6 10.4 copy-start.21
  424.7 10.4 copy-start.26
  435.1 12.6 copy-start.5
  435.1 12.6 copy-start.7
  435.1 12.6 copy-start.28
  447.7 177.2 %copy-start.27 = (f32[256]{0:T(256)S(1)}, f32[256]{0:T(256)}, u32[]{:S(2)}) copy-start(f32[256]{0:T(256)} %param.30) | copy-start | bytes 3076
  624.9 6.0 copy-start.10
  630.8 7.0 copy-start.29
  632.2 31.7 %all-to-all-start.1 = ((bf16[3,16,64,256]{3,1,0,2:T(8,128)(2,1)}), bf16[3,16,64,256]{3,1,0,2:T(8,128)(2,1)}, u32[]{:S(2)}, u32[]{:S(2)}) async-start(bf16[3,16,64,256]{3,1,0,2:T(8,128)(2,1)} %bitcast.114), calls=%async_computation.1 | async-start | bytes 3145728 | tf_op jit(solution)/shard_map/all_to_all | solution.py:115
  637.8 1666.1 %all-reduce.8.cloned.1.call-start = ((), (), s32[]{:S(2)}) async-start(), calls=%async_computation.3 | async-start | bytes 12582912
  1291.1 2.6 copy-start.1
  1291.1 0.8 copy-start.20
  1291.6 3.8 copy-start.8
  1293.7 1.7 copy-start.3
  1644.0 3.6 copy-start.32
Sparse Core Ops, SparseCore 0:
  631.0 655.7 all-reduce.5
  1647.8 656.0 all-reduce.7
where the time goes:
time: 2310 us
  waiting for transfers between devices  1300 us (56%)
  blocking collectives  866 us (37%)
  matrix products  68.9 us (3%)
  local copies, waits for them, and re-layouts  24.7 us (1%)
    unnamed x3, waiting for transfers between devices  655 us
    psum x1, waiting for transfers between devices, shards(): lax.psum(jnp.dot(scaled, mix_weight, preferred_element_type=jnp.float32),...  620 us
    psum x1, blocking collectives, shards(): io_all = lax.psum(io_term, ('sample', 'tensor')).astype(jnp.bfloat16)  356 us
    psum x1, blocking collectives, shards(): pair_all = lax.psum(pair_term, ('sample', 'tensor')).astype(jnp.bfloat16)  338 us
    psum x1, blocking collectives, shards(): lax.psum(group_pick * square_sum[:, None], ('sample', 'tensor'))  172 us
  transfers between devices with their start and end apart: 4, of which 3 were waited for; matrix products, arithmetic and copies ran while one was open for 1% of the time, Pallas kernels for 0%

commit v1 on v0

v1 whole, which is shorter than its diff:
```python
import jax
import jax.numpy as jnp
from jax import lax
from jax.experimental import pallas as pl
from jax.experimental.pallas import tpu as pltpu
from jax.sharding import PartitionSpec as P

F32 = jnp.float32
BF16 = jnp.bfloat16
MESH = pl.DeviceIdType.MESH
HIGH = lax.Precision.HIGHEST

STAGES = (
    "wio",
    "st1",
    "kvw",
    "ca1",
    "st2",
    "ca2",
    "iors",
    "ioag",
    "sq",
    "gm",
    "a1",
    "b1",
    "a2",
    "b2",
    "rz",
    "sq2",
    "sqy",
    "ma1",
    "mb1",
    "ma2",
    "mb2",
    "q",
    "kvr",
    "kva",
    "at",
    "c1",
    "d1",
    "c2",
    "d2",
    "sz",
    "fin",
    "w",
    "loc",
    "pro",
    "a1x",
    "b1x",
    "a2x",
    "b2x",
    "ma1x",
    "mb1x",
    "ma2x",
    "mb2x",
    "c1x",
    "d1x",
    "c2x",
    "d2x",
)
STAGE = {name: number for number, name in enumerate(STAGES)}


def nt_dot(left, right, precision=None):
    return lax.dot_general(
        left, right, (((1,), (1,)), ((), ())), preferred_element_type=F32, precision=precision
    )


def row_sums(values):
    ones = jnp.ones((8, values.shape[1]), F32)
    return nt_dot(ones, values * values, HIGH)


def to_column(rows):
    size = rows.shape[1]
    eye = (
        lax.broadcasted_iota(jnp.int32, (size, size), 0)
        == lax.broadcasted_iota(jnp.int32, (size, size), 1)
    ).astype(F32)
    return nt_dot(eye, rows, HIGH)[:, :1]


def kernel(
    lens,
    hid_h,
    st_h,
    cache_h,
    gain1,
    wg_h,
    wi_h,
    wrt,
    rate_bias,
    decay_log,
    skip_gain,
    mix_gain,
    wio_h,
    wm_h,
    gain2,
    wq_h,
    wkv_h,
    wo_h,
    out,
    hid,
    nrm,
    wg,
    wi,
    wm,
    wq,
    wo,
    wio,
    kvw,
    st1,
    st2,
    ca1,
    ca2,
    accg,
    acci,
    accr,
    nio,
    iop,
    ior,
    iog,
    sq,
    gm,
    part,
    ra1,
    rb1,
    qa,
    qb,
    ra2,
    rb2,
    rzs,
    rzr,
    res,
    sq2,
    sqy,
    mid,
    qs,
    qr,
    kvp,
    kvr,
    kvg,
    scores,
    os,
    orr,
    att,
    part2,
    rc1,
    rd1,
    qc,
    qd,
    rc2,
    rd2,
    szs,
    szr,
    fin,
    fo,
    fi,
    ssem,
    rsem,
):
    s = lax.axis_index("sample")
    t = lax.axis_index("tensor")
    z = lax.div(s, 16)
    y = lax.rem(lax.div(s, 4), 4)
    x = lax.rem(s, 4)
    g = lax.div(s, 4)
    i = 2 * x + t

    def al(value, size):
        return pl.multiple_of(value, size)

    def dev(sample, tensor):
        return {"sample": sample, "tensor": tensor}

    def dev_big_x(j):
        return dev(4 * g + lax.div(j, 2), lax.rem(j, 2))

    def dev_big_y(j):
        return dev(4 * j + x, t)

    def dev_x(j):
        return dev(4 * g + j, t)

    def dev_y(j):
        return dev(16 * z + 4 * j + x, t)

    sibling = dev(s, 1 - t)
    zpeer = dev(16 * (1 - z) + 4 * y + x, t)

    def remote(src, dst, stage, send_slot, recv_slot, device):
        return pltpu.make_async_remote_copy(
            src_ref=src,
            dst_ref=dst,
            send_sem=ssem.at[STAGE[stage], send_slot],
            recv_sem=rsem.at[STAGE[stage], recv_slot],
            device_id=device,
            device_id_type=MESH,
        )

    def local(src, dst, stage, slot):
        return pltpu.make_async_copy(src, dst, rsem.at[STAGE[stage], slot])

    pending = {}
    finish = []

    def exchange(stage, size, me, device, src_of, dst_of, own=False):
        def send(k, _):
            j = lax.rem(me + k, size)
            remote(src_of(j), dst_of(me), stage, j, me, device(j)).start()
            return 0

        def received(k, _):
            j = lax.rem(me + k, size)
            local(dst_of(j), dst_of(j), stage, j).wait()
            return 0

        def sent(k, _):
            j = lax.rem(me + k, size)
            pltpu.make_async_copy(src_of(j), src_of(j), ssem.at[STAGE[stage], j]).wait()
            return 0

        if own:
            local(src_of(me), dst_of(me), stage, me).start()
        lax.fori_loop(1, size, send, 0)
        pending[stage] = lambda: lax.fori_loop(0 if own else 1, size, received, 0)
        finish.append(lambda: lax.fori_loop(1, size, sent, 0))

    def swap(stage, src, dst, device, slot=0):
        copy = remote(src, dst, stage, slot, slot, device)
        copy.start()
        pending[stage, slot] = copy.wait_recv
        finish.append(copy.wait_send)

    def fetch(stage, src, dst, slot):
        copy = local(src, dst, stage, slot)
        copy.start()
        pending[stage, slot] = copy.wait

    def arrive(*names):
        for name in names:
            pending.pop(name)()

    def drain():
        for name in list(pending):
            arrive(name)
        for wait in finish:
            wait()

    fetch("loc", hid_h, hid, 0)

    def proj_copy(c, src, dst, slot):
        rows = pl.ds(al(c * 1024, 1024), 1024)
        return local(src.at[rows], dst.at[rows], "pro", 2 * c + slot)

    def start_proj(c, _):
        proj_copy(c, wg_h, wg, 0).start()
        proj_copy(c, wi_h, wi, 1).start()
        return 0

    lax.fori_loop(0, 8, start_proj, 0)

    def project_wait(c, _):
        proj_copy(c, wg_h, wg, 0).wait()
        proj_copy(c, wi_h, wi, 1).wait()
        return 0

    pending["pro"] = lambda: lax.fori_loop(0, 8, project_wait, 0)

    barrier = pltpu.get_barrier_semaphore()
    me = 2 * s + t

    def greet(k, _):
        j = lax.rem(me + k, 64)
        pl.semaphore_signal(
            barrier, inc=1, device_id=dev(lax.div(j, 2), lax.rem(j, 2)), device_id_type=MESH
        )
        return 0

    lax.fori_loop(1, 64, greet, 0)
    pl.semaphore_wait(barrier, 63)

    def wio_src(j):
        return wio_h.at[:, pl.ds(al(512 * j, 512), 512)]

    exchange("ca1", 8, g, dev_big_y, lambda j: cache_h.at[j], lambda j: ca1.at[:, j], own=True)
    exchange("st1", 8, i, dev_big_x, lambda j: st_h.at[j], lambda j: st1.at[j], own=True)
    exchange("wio", 8, g, dev_big_y, wio_src, lambda j: wio.at[j], own=True)

    half = al(4096 * t, 4096)
    other = al(4096 * (1 - t), 4096)
    own_rows = pl.ds(al(256 * t, 256), 256)
    head_rows = pl.ds(al(128 * t, 128), 128)
    fetch("loc", wm_h.at[:, pl.ds(half, 4096)], wm.at[own_rows], 1)
    swap("w", wm_h.at[:, pl.ds(other, 4096)], wm.at[own_rows], sibling, 0)
    fetch("loc", wq_h.at[pl.ds(half, 4096)], wq.at[:, head_rows], 2)
    swap("w", wq_h.at[pl.ds(other, 4096)], wq.at[:, head_rows], sibling, 1)
    fetch("loc", wo_h.at[:, pl.ds(half, 4096)], wo.at[head_rows], 3)
    swap("w", wo_h.at[:, pl.ds(other, 4096)], wo.at[head_rows], sibling, 2)

    arrive(("loc", 0))

    def norm_rows(r, _):
        rows = pl.ds(al(16 * r, 16), 16)
        values = hid[rows, :].astype(F32)
        scale = lax.rsqrt(jnp.mean(values * values, axis=1, keepdims=True) + 1e-05)
        nrm[rows, :] = (values * scale * gain1[...]).astype(BF16)
        return 0

    lax.fori_loop(0, 12, norm_rows, 0)
    arrive("ca1")
    exchange("ca2", 4, x, dev_x, lambda j: ca1, lambda j: ca2.at[j], own=True)

    accg[...] = jnp.zeros_like(accg)
    acci[...] = jnp.zeros_like(acci)
    accr[...] = jnp.zeros_like(accr)

    pending.pop("pro")

    def project(c, _):
        project_wait(c, 0)
        span = pl.ds(al(c * 1024, 1024), 1024)
        left = nrm[:, span]
        accg[...] += jnp.dot(left, wg[span, :], preferred_element_type=F32)
        acci[...] += jnp.dot(left, wi[span, :], preferred_element_type=F32)
        accr[...] += nt_dot(left, wrt[:, span])
        return 0

    lax.fori_loop(0, 8, project, 0)

    def pick(c, _):
        nio[:, pl.ds(al(128 * c, 128), 128)] = nrm[:, pl.ds(al(128 * (8 * c + i), 128), 128)]
        return 0

    lax.fori_loop(0, 8, pick, 0)
    arrive("wio", "st1")
    exchange("st2", 8, g, dev_big_y, lambda j: st1.at[:, j], lambda j: st2.at[j], own=True)
    io_part = jnp.dot(nio[...], wio[...].reshape(1024, 512), preferred_element_type=F32)
    for j in range(8):
        iop[j] = io_part[24 * j : 24 * j + 24]
    exchange("iors", 8, i, dev_big_x, lambda j: iop.at[j], lambda j: ior.at[j])
    arrive("iors")
    io_sum = iop[i]
    for k in range(1, 8):
        io_sum = io_sum + ior[lax.rem(i + k, 8)]
    iog[i] = io_sum.astype(BF16)
    exchange("ioag", 8, i, dev_big_x, lambda j: iog.at[i], lambda j: iog.at[j])

    lift = (
        lax.broadcasted_iota(jnp.int32, (4, 256), 0)
        == lax.div(lax.broadcasted_iota(jnp.int32, (4, 256), 1), 64)
    ).astype(F32)

    def widen(heads):
        return jnp.dot(heads, lift, preferred_element_type=F32, precision=HIGH)

    raw = widen(accr[...] + rate_bias[...])
    rate = jnp.maximum(raw, 0.0) + jnp.log1p(jnp.exp(-jnp.abs(raw)))
    decay = jnp.exp(rate * -jnp.exp(widen(decay_log[...])))
    skip = widen(skip_gain[...])
    entering = rate * acci[...]
    column = lax.broadcasted_iota(jnp.int32, (256, 1024), 1)
    inside = lax.rem(column, 16)
    owner = lax.div(column, 16)
    spread = (
        (4 * owner + lax.rem(inside, 4) == lax.broadcasted_iota(jnp.int32, (256, 1024), 0))
        & (inside < 12)
    )
    spread = jnp.where(spread, 1.0, 0.0).astype(BF16)

    arrive("ioag")
    def kvw_src(j):
        return wkv_h.at[:, pl.ds(al(256 * j, 256), 256)]

    kvw_slot = 2 * y + t

    def kvw_copy(j):
        return remote(kvw_src(j), kvw.at[kvw_slot], "kvw", j, kvw_slot, dev(4 * j + x, z))

    def kvw_send(k, _):
        kvw_copy(lax.rem(g + k, 8)).start()
        return 0

    lax.fori_loop(1, 8, kvw_send, 0)

    @pl.when(t == z)
    def _():
        local(kvw_src(g), kvw.at[kvw_slot], "kvw", kvw_slot).start()

    @pl.when(t != z)
    def _():
        kvw_copy(g).start()

    def kvw_received(k, _):
        local(kvw.at[k], kvw.at[k], "kvw", k).wait()
        return 0

    def kvw_sent(k, _):
        kvw_copy(lax.rem(g + k, 8)).wait_send()
        return 0

    def kvw_finish():
        lax.fori_loop(1, 8, kvw_sent, 0)

        @pl.when(t != z)
        def _():
            kvw_copy(g).wait_send()

    pending["kvw"] = lambda: lax.fori_loop(0, 8, kvw_received, 0)
    finish.append(kvw_finish)
    io_all = jnp.concatenate([iog[j].astype(F32) for j in range(8)], axis=0)
    in_vec = io_all[:, :256]
    out_vec = io_all[:, 256:]
    wide = jnp.dot(out_vec.astype(BF16), spread, preferred_element_type=F32)
    row_prompt = lax.rem(lax.div(lax.broadcasted_iota(jnp.int32, (192, 1024), 0), 16), 3)
    col_prompt = lax.div(
        lax.rem(lax.broadcasted_iota(jnp.int32, (192, 1024), 1), 16), 4
    )
    wide = jnp.where(row_prompt == col_prompt, wide, 0.0).astype(BF16)
    arrive("st2")
    start = jnp.dot(wide, st2[...].reshape(1024, 256), preferred_element_type=F32)

    mixed = []
    running = None
    carried = []
    for step in range(4):
        rows = slice(48 * step, 48 * step + 48)
        fall = decay[rows]
        running = fall if running is None else running * fall
        carried = [term * fall for term in carried] + [entering[rows]]
        value = running * start[rows]
        for earlier in range(step + 1):
            match = jnp.sum(
                out_vec[rows] * in_vec[48 * earlier : 48 * earlier + 48], axis=1, keepdims=True
            )
            value = value + match * carried[earlier]
        mixed.append(value + skip * acci[rows, :])
    gate = accg[...]
    gated = jnp.concatenate(mixed, axis=0) * (gate / (1.0 + jnp.exp(-gate)))
    gm[:, own_rows] = (gated * mix_gain[...]).astype(BF16)
    swap("gm", gm.at[:, own_rows], gm.at[:, own_rows], sibling)
    sq[i] = row_sums(gated)
    exchange("sq", 8, i, dev_big_x, lambda j: sq.at[i], lambda j: sq.at[j])
    arrive("sq")
    group_sum = sq[0]
    for j in range(1, 8):
        group_sum = group_sum + sq[j]
    inverse = to_column(lax.rsqrt(group_sum * (1.0 / 2048.0) + 1e-05))
    arrive(("gm", 0), ("loc", 1), ("w", 0))

    my_rows = pl.ds(al(48 * y, 48), 48)
    low = pl.ds(0, 256)
    high = pl.ds(256, 256)

    def rows_of(j):
        return pl.ds(al(48 * j, 48), 48)

    def reduce_scatter(names, left, weight, column, p, a1, b1, sa, sb, a2, b2, zs, zr, use):
        na1, nb1, na2, nb2, nz = names
        tails = ("", "x")

        for c in range(2):

            def block(n, _, c=c):
                xx = lax.div(n, 2)
                hh = lax.rem(n, 2)
                cols = pl.ds(al(1024 * xx + 512 * hh + 256 * c, 256), 256)
                value = jnp.dot(left[...], weight[:, cols], preferred_element_type=F32)
                if column is not None:
                    value = value * column
                p[c, xx, :, pl.ds(al(256 * hh, 256), 256)] = value.astype(BF16)
                return 0

            lax.fori_loop(0, 8, block, 0)
            exchange(
                na1 + tails[c],
                4,
                y,
                dev_y,
                lambda j, c=c: p.at[c, :, rows_of(j), low],
                lambda j, c=c: a1.at[c, j],
            )
            exchange(
                nb1 + tails[c],
                4,
                x,
                dev_x,
                lambda j, c=c: p.at[c, j, :, high],
                lambda j, c=c: b1.at[c, j],
            )
        for c in range(2):
            arrive(na1 + tails[c])
            for xx in range(4):
                total = p[c, xx, my_rows, 0:256].astype(F32)
                for k in range(1, 4):
                    total = total + a1[c, lax.rem(y + k, 4), xx].astype(F32)
                sa[c, xx] = total.astype(BF16)
            exchange(
                na2 + tails[c],
                4,
                x,
                dev_x,
                lambda j, c=c: sa.at[c, j],
                lambda j, c=c: a2.at[c, j],
            )
            arrive(nb1 + tails[c])
            total = p[c, x, :, 256:512].astype(F32)
            for k in range(1, 4):
                total = total + b1[c, lax.rem(x + k, 4)].astype(F32)
            sb[c] = total.astype(BF16)
            exchange(
                nb2 + tails[c],
                4,
                y,
                dev_y,
                lambda j, c=c: sb.at[c, rows_of(j)],
                lambda j, c=c: b2.at[c, j],
            )
        for c in range(2):
            arrive(na2 + tails[c])
            total = sa[c, x].astype(F32)
            for k in range(1, 4):
                total = total + a2[c, lax.rem(x + k, 4)].astype(F32)
            zs[c, :, 0:256] = total.astype(BF16)
            arrive(nb2 + tails[c])
            total = sb[c, my_rows, :].astype(F32)
            for k in range(1, 4):
                total = total + b2[c, lax.rem(y + k, 4)].astype(F32)
            zs[c, :, 256:512] = total.astype(BF16)
            swap(nz, zs.at[c], zr.at[c], zpeer, c)
        for c in range(2):
            arrive((nz, c))
            use(c, zs[c].astype(F32) + zr[c].astype(F32))

    feature = al(1024 * (4 * t + x), 1024)
    squares = []

    def use_mix(c, value):
        spans = [al(feature + 256 * c, 256), al(feature + 512 + 256 * c, 256)]
        old = jnp.concatenate([hid[my_rows, pl.ds(span, 256)] for span in spans], axis=1)
        gain = jnp.concatenate([gain2[:, pl.ds(span, 256)] for span in spans], axis=1)
        residual = old.astype(F32) + value
        res[c] = residual
        mid[c, x, my_rows, :] = (residual * gain).astype(BF16)
        tail = ("", "x")[c]
        exchange(
            "ma1" + tail,
            4,
            x,
            dev_x,
            lambda j: mid.at[c, x, my_rows, low],
            lambda j: mid.at[c, j, my_rows, low],
        )
        exchange(
            "mb1" + tail,
            4,
            y,
            dev_y,
            lambda j: mid.at[c, x, my_rows, high],
            lambda j: mid.at[c, x, rows_of(j), high],
        )
        squares.append(row_sums(residual))

    reduce_scatter(
        ("a1", "b1", "a2", "b2", "rz"),
        gm,
        wm,
        inverse,
        part,
        ra1,
        rb1,
        qa,
        qb,
        ra2,
        rb2,
        rzs,
        rzr,
        use_mix,
    )
    sq2[i] = squares[0] + squares[1]
    exchange("sq2", 8, i, dev_big_x, lambda j: sq2.at[i], lambda j: sq2.at[j])
    for c in range(2):
        tail = ("", "x")[c]
        arrive("ma1" + tail)
        exchange(
            "ma2" + tail,
            4,
            y,
            dev_y,
            lambda j, c=c: mid.at[c, :, my_rows, low],
            lambda j, c=c: mid.at[c, :, rows_of(j), low],
        )
        arrive("mb1" + tail)
        exchange(
            "mb2" + tail,
            4,
            x,
            dev_x,
            lambda j, c=c: mid.at[c, x, :, high],
            lambda j, c=c: mid.at[c, j, :, high],
        )
    arrive("sq2")
    row_sum = sq2[0]
    for j in range(1, 8):
        row_sum = row_sum + sq2[j]
    sqy[y] = row_sum
    exchange("sqy", 4, y, dev_y, lambda j: sqy.at[y], lambda j: sqy.at[j])
    arrive("sqy")
    scale = jnp.concatenate(
        [to_column(lax.rsqrt(sqy[j] * (1.0 / 8192.0) + 1e-05)) for j in range(4)], axis=0
    )

    arrive(("loc", 2), ("w", 1), "kvw")
    query = jnp.zeros((192, 256), F32)
    pair = jnp.zeros((192, 256), F32)
    for c in range(2):
        tail = ("", "x")[c]
        arrive("ma2" + tail, "mb2" + tail)
        for xx in range(4):
            for hh in range(2):
                place = 1024 * xx + 512 * hh + 256 * c
                query = query + jnp.dot(
                    mid[c, xx, :, 256 * hh : 256 * hh + 256],
                    wq[place : place + 256, :],
                    preferred_element_type=F32,
                )
    for xx in range(4):
        pair = pair + jnp.dot(
            mid[lax.rem(x, 2), xx, :, pl.ds(al(256 * lax.div(x, 2), 256), 256)],
            kvw[2 * xx : 2 * xx + 2].reshape(256, 256),
            preferred_element_type=F32,
        )
    pair = pair * scale
    for j in range(8):
        kvp[j] = pair[24 * j : 24 * j + 24]
    exchange("kvr", 8, i, dev_big_x, lambda j: kvp.at[j], lambda j: kvr.at[j])
    qs[...] = query
    swap("q", qs, qr, sibling)

    arrive("kvr")
    pair_sum = kvp[i]
    for k in range(1, 8):
        pair_sum = pair_sum + kvr[lax.rem(i + k, 8)]
    kvg[i] = pair_sum.astype(BF16)
    exchange("kva", 8, i, dev_big_x, lambda j: kvg.at[i], lambda j: kvg.at[j])

    arrive(("q", 0))
    query_rows = ((qs[...] + qr[...]) * (scale * (128.0**-0.5))).astype(BF16)
    arrive("ca2")
    query_of = []
    lane = lax.broadcasted_iota(jnp.int32, (128, 128), 1)
    place = 128 * lax.div(lane, 16) + lax.rem(lane, 16) + 16 * t
    for p in range(3):
        query_p = jnp.concatenate(
            [
                query_rows[48 * step + 16 * p : 48 * step + 16 * p + 16, 128 * head : 128 * head + 128]
                for head in range(2)
                for step in range(4)
            ],
            axis=0,
        )
        query_of.append(query_p)
        for j in range(4):
            keys = ca2[j, p, :, :, 0:128].reshape(128, 128)
            score = nt_dot(query_p, keys)
            scores[p, :, 128 * j : 128 * j + 128] = jnp.where(
                place + 32 * j < lens[p], score, -1e30
            )

    arrive("kva")
    pair_all = jnp.concatenate([kvg[j].astype(F32) for j in range(8)], axis=0)
    row_step = lax.rem(lax.div(lax.broadcasted_iota(jnp.int32, (128, 1), 0), 16), 4)
    row_step = row_step - 4 * t
    wide_lane = lax.broadcasted_iota(jnp.int32, (128, 128), 1)
    for p in range(3):
        far = scores[p]
        top = jnp.max(far, axis=1, keepdims=True)
        near = []
        values = []
        query_p = query_of[p].astype(F32)
        for step in range(4):
            block = pair_all[48 * step + 16 * p : 48 * step + 16 * p + 16]
            tiled = jnp.concatenate([block] * 8, axis=0)
            values.append(tiled[:, 128:])
            score = jnp.sum(query_p * tiled[:, :128], axis=1, keepdims=True)
            score = jnp.where(row_step >= step, score, -1e30)
            near.append(score)
            top = jnp.maximum(top, score)
        far = jnp.exp(far - top)
        near = [jnp.exp(score - top) for score in near]
        total = jnp.sum(far, axis=1, keepdims=True)
        for weight in near:
            total = total + weight
        far = far.astype(BF16)
        result = jnp.zeros((128, 128), F32)
        for j in range(4):
            result = result + jnp.dot(
                far[:, 128 * j : 128 * j + 128],
                ca2[j, p, :, :, 128:256].reshape(128, 128),
                preferred_element_type=F32,
            )
        for weight, value in zip(near, values):
            result = result + weight.astype(BF16).astype(F32) * value
        os[p, :, 0:128] = result
        os[p, :, 128:256] = jnp.where(wide_lane < 64, top, total)
        swap("at", os.at[p], orr.at[p], sibling, p)
    for p in range(3):
        arrive(("at", p))
        mine_top, mine_total = os[p, :, 128:129], os[p, :, 192:193]
        peer_top, peer_total = orr[p, :, 128:129], orr[p, :, 192:193]
        top = jnp.maximum(mine_top, peer_top)
        mine = jnp.exp(mine_top - top)
        peer = jnp.exp(peer_top - top)
        total = mine_total * mine + peer_total * peer
        result = (os[p, :, 0:128] * (mine / total) + orr[p, :, 0:128] * (peer / total)).astype(BF16)
        for head in range(2):
            for step in range(4):
                att[48 * step + 16 * p : 48 * step + 16 * p + 16, 128 * head : 128 * head + 128] = (
                    result[64 * head + 16 * step : 64 * head + 16 * step + 16]
                )

    arrive(("loc", 3), ("w", 2))

    def use_out(c, value):
        value = res[c] + value
        fin[0:48, 256 * c : 256 * c + 256] = value[:, 0:256]
        fin[0:48, 512 + 256 * c : 768 + 256 * c] = value[:, 256:512]

    reduce_scatter(
        ("c1", "d1", "c2", "d2", "sz"),
        att,
        wo,
        None,
        part2,
        rc1,
        rd1,
        qc,
        qd,
        rc2,
        rd2,
        szs,
        szr,
        use_out,
    )

    fin[48:56, :] = jnp.zeros((8, 1024), F32)
    sends = lax.div(y, 2) == z

    def fin_copy(k):
        target = 16 * y + k
        return remote(
            fo.at[k], fi.at[i], "fin", k, i, dev(lax.div(target, 2), lax.rem(target, 2))
        )

    @pl.when(sends)
    def _():
        for k in range(16):
            fo[k] = fin[3 * k : 3 * k + 8, :].astype(BF16)

        def send(k, _):
            @pl.when(16 * y + k == me)
            def _():
                local(fo.at[k], fi.at[i], "fin", i).start()

            @pl.when(16 * y + k != me)
            def _():
                fin_copy(k).start()

            return 0

        lax.fori_loop(0, 16, send, 0)

    def fin_received(k, _):
        local(fi.at[k], fi.at[k], "fin", k).wait()
        return 0

    def fin_finish():
        @pl.when(sends)
        def _():
            def sent(k, _):
                @pl.when(16 * y + k != me)
                def _():
                    fin_copy(k).wait_send()

                return 0

            lax.fori_loop(0, 16, sent, 0)

    lax.fori_loop(0, 8, fin_received, 0)
    finish.append(fin_finish)
    for j in range(8):
        place_j = 1024 * (4 * (j % 2) + j // 2)
        out[:, place_j : place_j + 1024] = fi[j][0:3, :]
    drain()


def scratch():
    def v(shape, dtype=BF16):
        return pltpu.VMEM(shape, dtype)

    reduce_bufs = [
        v((2, 4, 4, 48, 256)),
        v((2, 4, 192, 256)),
        v((2, 4, 48, 256)),
        v((2, 192, 256)),
        v((2, 4, 48, 256)),
        v((2, 4, 48, 256)),
        v((2, 48, 512)),
        v((2, 48, 512)),
    ]
    return [
        v((192, 8192)),
        v((192, 8192)),
        v((8192, 256)),
        v((8192, 256)),
        v((512, 4096)),
        v((4096, 256)),
        v((256, 4096)),
        v((8, 128, 512)),
        v((8, 128, 256)),
        v((8, 8, 16, 256)),
        v((8, 8, 16, 256)),
        v((3, 8, 16, 256)),
        v((4, 3, 8, 16, 256)),
        v((192, 256), F32),
        v((192, 256), F32),
        v((192, 4), F32),
        v((192, 1024)),
        v((8, 24, 512), F32),
        v((8, 24, 512), F32),
        v((8, 24, 512)),
        v((8, 8, 192), F32),
        v((192, 512)),
        v((2, 4, 192, 512)),
        *reduce_bufs,
        v((2, 48, 512), F32),
        v((8, 8, 48), F32),
        v((4, 8, 48), F32),
        v((2, 4, 192, 512)),
        v((192, 256), F32),
        v((192, 256), F32),
        v((8, 24, 256), F32),
        v((8, 24, 256), F32),
        v((8, 24, 256)),
        v((3, 128, 512), F32),
        v((3, 128, 256), F32),
        v((3, 128, 256), F32),
        v((192, 256)),
        v((2, 4, 192, 512)),
        *reduce_bufs,
        v((56, 1024), F32),
        v((16, 8, 1024)),
        v((8, 8, 1024)),
        pltpu.SemaphoreType.DMA((len(STAGES), 16)),
        pltpu.SemaphoreType.DMA((len(STAGES), 16)),
    ]


def shards(
    hidden_input,
    prompt_lengths,
    prompt_states,
    prompt_cache,
    input_gain,
    gate_weight,
    input_weight,
    rate_weight,
    rate_bias,
    decay_log,
    skip_gain,
    state_io_weight,
    mix_gain,
    mix_weight,
    middle_gain,
    query_weight,
    key_value_weight,
    output_weight,
):
    hidden = hidden_input.reshape(192, 8192)
    states = jnp.pad(prompt_states.astype(BF16), ((0, 1), (0, 0), (0, 0), (0, 0)))
    states = states.reshape(4, 8, 8, 4, 64, 4).transpose(2, 1, 0, 5, 3, 4).reshape(8, 8, 16, 256)
    cache = prompt_cache.transpose(2, 0, 1, 3)
    vmem = pl.BlockSpec(memory_space=pltpu.VMEM)
    smem = pl.BlockSpec(memory_space=pltpu.SMEM)
    anyw = pl.BlockSpec(memory_space=pl.ANY)
    return pl.pallas_call(
        kernel,
        out_shape=jax.ShapeDtypeStruct((3, 8192), BF16),
        in_specs=[
            smem,
            anyw,
            anyw,
            anyw,
            vmem,
            anyw,
            anyw,
            vmem,
            vmem,
            vmem,
            vmem,
            vmem,
            anyw,
            anyw,
            vmem,
            anyw,
            anyw,
            anyw,
        ],
        out_specs=vmem,
        scratch_shapes=scratch(),
        compiler_params=pltpu.CompilerParams(
            collective_id=0, has_side_effects=True, vmem_limit_bytes=60 * 1024 * 1024
        ),
        cost_estimate=pl.CostEstimate(
            flops=4_000_000_000, bytes_accessed=24_000_000, transcendentals=1_000_000
        ),
    )(
        prompt_lengths,
        hidden,
        states,
        cache,
        input_gain[None, :],
        gate_weight,
        input_weight,
        rate_weight.T,
        rate_bias[None, :],
        decay_log[None, :],
        skip_gain[None, :],
        mix_gain[None, :],
        state_io_weight,
        mix_weight,
        middle_gain[None, :],
        query_weight,
        key_value_weight,
        output_weight,
    )


def solution(mesh):
    in_specs = (
        P(None, "prompt", None),
        P("prompt"),
        P("prompt", None, None, ("sample", "tensor")),
        P("prompt", ("sample", "tensor"), None, None),
        P(),
        P(None, ("sample", "tensor")),
        P(None, ("sample", "tensor")),
        P(None, ("sample", "tensor")),
        P(("sample", "tensor")),
        P(("sample", "tensor")),
        P(("sample", "tensor")),
        P(("sample", "tensor"), None),
        P(("sample", "tensor")),
        P(("sample", "tensor"), None),
        P(),
        P(None, ("sample", "tensor")),
        P(("sample", "tensor"), None),
        P(("sample", "tensor"), None),
    )
    out_specs = P(("prompt", "sample", "tensor"), None)
    return jax.shard_map(shards, mesh=mesh, in_specs=in_specs, out_specs=out_specs, check_vma=False)
```

time: 2310 us -> 138 us (0.06)
  waiting for transfers between devices: 1300 us -> 0 us
  blocking collectives: 866 us -> 0 us
  Pallas kernels: 0 us -> 132 us
  matrix products: 68.9 us -> 0 us
    psum x3 -> x0, blocking collectives: 866 us -> none  [the longest x1 356 us: shards(): io_all = lax.psum(io_term, ('sample', 'tensor')).astype(jnp.bfloat16)]
    unnamed x3 -> x0, waiting for transfers between devices: 655 us -> none
    psum x1 -> x0, waiting for transfers between devices: 620 us -> none  [shards(): lax.psum(jnp.dot(scaled, mix_weight, preferred_element_type=jnp.float32),...]
    pallas_call x0 -> x1, Pallas kernels: none -> 132 us  [shards(): pl.pallas_call(kernel, out_shape=jax.ShapeDtypeStruct((3, 8192), BF16), i...]
    dot_general x16 -> x0, matrix products: 68.9 us -> none  [the longest x4 38.2 us: shards(): jnp.einsum('rhdn,rn->rhd', carried, io_steps[moment][:, state_size:], pre...]
    all_to_all x2 -> x0, waiting for transfers between devices: 26 us -> none  [the longest x1 26 us: shards(): lax.all_to_all(spread, ('sample', 'tensor'), split_axis=2, concat_axis=1,...]
  transfers between devices with their start and end apart: 4 -> 0, of which waited for: 3 -> 0; matrix products, arithmetic and copies ran while one was open for 1% -> 0% of each run, Pallas kernels for 0% -> 0%
where the time goes in v1:
time: 138 us
  Pallas kernels  132 us (96%)
  local copies, waits for them, and re-layouts  5.83 us (4%)
    pallas_call x1, Pallas kernels, shards(): pl.pallas_call(kernel, out_shape=jax.ShapeDtypeStruct((3, 8192), BF16), i...  132 us
    unnamed x6, local copies, waits for them, and re-layouts  3.87 us

profile of v1, /device:TPU:1, one launch (start us, length us, event | category | flops | bytes accessed | tf_op | source)
XLA Modules:
  0.0 137.6 jit_solution(1787944056041830891)
XLA Ops:
  0.0 0.0 copy-start
  0.0 1.3 copy.32
  1.3 0.4 copy.29
  1.7 0.2 pad.4.clone
  1.9 0.7 reshape.12
  2.6 1.1 copy.28.st_h
  3.6 0.0 copy-done
  3.7 0.7 copy.33
  4.4 131.7 %shard_map.172 = bf16[3,8192]{1,0:T(4,128)(2,1)} custom-call(s32[3]{0:T(128)} %lens.1, bf16[192,8192]{1,0:T(8,128)(2,1)} %bitcast.17, bf16[8,8,16,256]{3,2,1,0:T(8,128)(2,1)} %copy.28.st_h, bf16[8,3,16,256]{3,2,1,0:T(8,128)(2,1)} %bitcast.18, f32[1,8192]{1,0:T(1,128)} %bitcast.20, bf16[8192,256]{1,0:T(8,128)(2,1)} %wg_h.1, bf16[8192,256]{1,0:T(8,128)(2,1)} %wi_h.1, ...), custom_call_target="tpu_custom_call" | custom-call | flops 4000000000 | bytes 24000000 | tf_op jit(solution)/shard_map/pallas_call | solution.py:887
  136.1 1.5 %copy.35 = bf16[3,8192]{1,0:T(4,128)(2,1)} copy(bf16[3,8192]{1,0:T(4,128)(2,1)} %shard_map.172) | data formatting | bytes 98304
Async XLA Ops:
  0.0 3.7 %copy-start = (bf16[3,16,8,256]{3,2,1,0:T(8,128)(2,1)S(1)}, bf16[3,16,8,256]{3,2,1,0:T(8,128)(2,1)}, u32[]{:S(2)}) copy-start(bf16[3,16,8,256]{3,2,1,0:T(8,128)(2,1)} %param.21) | copy-start | bytes 589828

commit v2 on v1

--- a/solution.py
+++ b/solution.py
@@ -14,6 +14,7 @@
     "wio",
     "st1",
     "kvw",
+    "kvx",
     "ca1",
     "st2",
     "ca2",
@@ -25,7 +26,6 @@
     "b1",
     "a2",
     "b2",
-    "rz",
     "sq2",
     "sqy",
     "ma1",
@@ -35,16 +35,11 @@
     "q",
     "kvr",
     "kva",
-    "at",
     "c1",
     "d1",
     "c2",
     "d2",
-    "sz",
     "fin",
-    "w",
-    "loc",
-    "pro",
     "a1x",
     "b1x",
     "a2x",
@@ -57,6 +52,21 @@
     "d1x",
     "c2x",
     "d2x",
+    "w0",
+    "w1",
+    "w2",
+    "loc0",
+    "loc1",
+    "loc2",
+    "loc3",
+    "rz0",
+    "rz1",
+    "sz0",
+    "sz1",
+    "at0",
+    "at1",
+    "at2",
+    "pro",
 )
 STAGE = {name: number for number, name in enumerate(STAGES)}
 
@@ -159,6 +169,7 @@
     fi,
     ssem,
     rsem,
+    psem,
 ):
     s = lax.axis_index("sample")
     t = lax.axis_index("tensor")
@@ -189,54 +200,49 @@
     sibling = dev(s, 1 - t)
     zpeer = dev(16 * (1 - z) + 4 * y + x, t)
 
-    def remote(src, dst, stage, send_slot, recv_slot, device):
+    def remote(src, dst, stage, device, landing=None):
         return pltpu.make_async_remote_copy(
             src_ref=src,
             dst_ref=dst,
-            send_sem=ssem.at[STAGE[stage], send_slot],
-            recv_sem=rsem.at[STAGE[stage], recv_slot],
+            send_sem=ssem.at[STAGE[stage]],
+            recv_sem=rsem.at[STAGE[landing or stage]],
             device_id=device,
             device_id_type=MESH,
         )
 
-    def local(src, dst, stage, slot):
-        return pltpu.make_async_copy(src, dst, rsem.at[STAGE[stage], slot])
+    def local(src, dst, stage):
+        return pltpu.make_async_copy(src, dst, rsem.at[STAGE[stage]])
+
+    def all_sent(ref, stage):
+        pltpu.make_async_copy(ref, ref, ssem.at[STAGE[stage]]).wait()
 
     pending = {}
     finish = []
 
-    def exchange(stage, size, me, device, src_of, dst_of, own=False):
+    def exchange(stage, size, me, device, src_of, dst_of, span, own=False):
         def send(k, _):
             j = lax.rem(me + k, size)
-            remote(src_of(j), dst_of(me), stage, j, me, device(j)).start()
+            remote(src_of(j), dst_of(me), stage, device(j)).start()
             return 0
 
-        def received(k, _):
-            j = lax.rem(me + k, size)
-            local(dst_of(j), dst_of(j), stage, j).wait()
-            return 0
-
-        def sent(k, _):
-            j = lax.rem(me + k, size)
-            pltpu.make_async_copy(src_of(j), src_of(j), ssem.at[STAGE[stage], j]).wait()
-            return 0
-
         if own:
-            local(src_of(me), dst_of(me), stage, me).start()
+            local(src_of(me), dst_of(me), stage).start()
         lax.fori_loop(1, size, send, 0)
-        pending[stage] = lambda: lax.fori_loop(0 if own else 1, size, received, 0)
-        finish.append(lambda: lax.fori_loop(1, size, sent, 0))
-
-    def swap(stage, src, dst, device, slot=0):
-        copy = remote(src, dst, stage, slot, slot, device)
+        landed = span(size if own else size - 1)
+        left = span(size - 1)
+        pending[stage] = local(landed, landed, stage).wait
+        finish.append(lambda: all_sent(left, stage))
+
+    def swap(stage, src, dst, device):
+        copy = remote(src, dst, stage, device)
         copy.start()
-        pending[stage, slot] = copy.wait_recv
+        pending[stage] = copy.wait_recv
         finish.append(copy.wait_send)
 
-    def fetch(stage, src, dst, slot):
-        copy = local(src, dst, stage, slot)
+    def fetch(stage, src, dst):
+        copy = local(src, dst, stage)
         copy.start()
-        pending[stage, slot] = copy.wait
+        pending[stage] = copy.wait
 
     def arrive(*names):
         for name in names:
@@ -248,25 +254,25 @@
         for wait in finish:
             wait()
 
-    fetch("loc", hid_h, hid, 0)
+    fetch("loc0", hid_h, hid)
 
     def proj_copy(c, src, dst, slot):
-        rows = pl.ds(al(c * 1024, 1024), 1024)
-        return local(src.at[rows], dst.at[rows], "pro", 2 * c + slot)
+        rows = pl.ds(al(c * 2048, 2048), 2048)
+        return pltpu.make_async_copy(src.at[rows], dst.at[rows], psem.at[2 * c + slot])
 
     def start_proj(c, _):
         proj_copy(c, wg_h, wg, 0).start()
         proj_copy(c, wi_h, wi, 1).start()
         return 0
 
-    lax.fori_loop(0, 8, start_proj, 0)
+    lax.fori_loop(0, 4, start_proj, 0)
 
     def project_wait(c, _):
         proj_copy(c, wg_h, wg, 0).wait()
         proj_copy(c, wi_h, wi, 1).wait()
         return 0
 
-    pending["pro"] = lambda: lax.fori_loop(0, 8, project_wait, 0)
+    pending["pro"] = lambda: lax.fori_loop(0, 4, project_wait, 0)
 
     barrier = pltpu.get_barrier_semaphore()
     me = 2 * s + t
@@ -284,22 +290,22 @@
     def wio_src(j):
         return wio_h.at[:, pl.ds(al(512 * j, 512), 512)]
 
-    exchange("ca1", 8, g, dev_big_y, lambda j: cache_h.at[j], lambda j: ca1.at[:, j], own=True)
-    exchange("st1", 8, i, dev_big_x, lambda j: st_h.at[j], lambda j: st1.at[j], own=True)
-    exchange("wio", 8, g, dev_big_y, wio_src, lambda j: wio.at[j], own=True)
+    exchange("ca1", 8, g, dev_big_y, lambda j: cache_h.at[j], lambda j: ca1.at[:, j], lambda n: ca1.at[:, pl.ds(0, n)], own=True)
+    exchange("st1", 8, i, dev_big_x, lambda j: st_h.at[j], lambda j: st1.at[j], lambda n: st1.at[pl.ds(0, n)], own=True)
+    exchange("wio", 8, g, dev_big_y, wio_src, lambda j: wio.at[j], lambda n: wio.at[pl.ds(0, n)], own=True)
 
     half = al(4096 * t, 4096)
     other = al(4096 * (1 - t), 4096)
     own_rows = pl.ds(al(256 * t, 256), 256)
     head_rows = pl.ds(al(128 * t, 128), 128)
-    fetch("loc", wm_h.at[:, pl.ds(half, 4096)], wm.at[own_rows], 1)
-    swap("w", wm_h.at[:, pl.ds(other, 4096)], wm.at[own_rows], sibling, 0)
-    fetch("loc", wq_h.at[pl.ds(half, 4096)], wq.at[:, head_rows], 2)
-    swap("w", wq_h.at[pl.ds(other, 4096)], wq.at[:, head_rows], sibling, 1)
-    fetch("loc", wo_h.at[:, pl.ds(half, 4096)], wo.at[head_rows], 3)
-    swap("w", wo_h.at[:, pl.ds(other, 4096)], wo.at[head_rows], sibling, 2)
-
-    arrive(("loc", 0))
+    fetch("loc1", wm_h.at[:, pl.ds(half, 4096)], wm.at[own_rows])
+    swap("w0", wm_h.at[:, pl.ds(other, 4096)], wm.at[own_rows], sibling)
+    fetch("loc2", wq_h.at[pl.ds(half, 4096)], wq.at[:, head_rows])
+    swap("w1", wq_h.at[pl.ds(other, 4096)], wq.at[:, head_rows], sibling)
+    fetch("loc3", wo_h.at[:, pl.ds(half, 4096)], wo.at[head_rows])
+    swap("w2", wo_h.at[:, pl.ds(other, 4096)], wo.at[head_rows], sibling)
+
+    arrive("loc0")
 
     def norm_rows(r, _):
         rows = pl.ds(al(16 * r, 16), 16)
@@ -310,7 +316,7 @@
 
     lax.fori_loop(0, 12, norm_rows, 0)
     arrive("ca1")
-    exchange("ca2", 4, x, dev_x, lambda j: ca1, lambda j: ca2.at[j], own=True)
+    exchange("ca2", 4, x, dev_x, lambda j: ca1, lambda j: ca2.at[j], lambda n: ca2.at[pl.ds(0, n)], own=True)
 
     accg[...] = jnp.zeros_like(accg)
     acci[...] = jnp.zeros_like(acci)
@@ -320,14 +326,14 @@
 
     def project(c, _):
         project_wait(c, 0)
-        span = pl.ds(al(c * 1024, 1024), 1024)
+        span = pl.ds(al(c * 2048, 2048), 2048)
         left = nrm[:, span]
         accg[...] += jnp.dot(left, wg[span, :], preferred_element_type=F32)
         acci[...] += jnp.dot(left, wi[span, :], preferred_element_type=F32)
         accr[...] += nt_dot(left, wrt[:, span])
         return 0
 
-    lax.fori_loop(0, 8, project, 0)
+    lax.fori_loop(0, 4, project, 0)
 
     def pick(c, _):
         nio[:, pl.ds(al(128 * c, 128), 128)] = nrm[:, pl.ds(al(128 * (8 * c + i), 128), 128)]
@@ -335,17 +341,17 @@
 
     lax.fori_loop(0, 8, pick, 0)
     arrive("wio", "st1")
-    exchange("st2", 8, g, dev_big_y, lambda j: st1.at[:, j], lambda j: st2.at[j], own=True)
+    exchange("st2", 8, g, dev_big_y, lambda j: st1.at[:, j], lambda j: st2.at[j], lambda n: st2.at[pl.ds(0, n)], own=True)
     io_part = jnp.dot(nio[...], wio[...].reshape(1024, 512), preferred_element_type=F32)
     for j in range(8):
         iop[j] = io_part[24 * j : 24 * j + 24]
-    exchange("iors", 8, i, dev_big_x, lambda j: iop.at[j], lambda j: ior.at[j])
+    exchange("iors", 8, i, dev_big_x, lambda j: iop.at[j], lambda j: ior.at[j], lambda n: ior.at[pl.ds(0, n)])
     arrive("iors")
     io_sum = iop[i]
     for k in range(1, 8):
         io_sum = io_sum + ior[lax.rem(i + k, 8)]
     iog[i] = io_sum.astype(BF16)
-    exchange("ioag", 8, i, dev_big_x, lambda j: iog.at[i], lambda j: iog.at[j])
+    exchange("ioag", 8, i, dev_big_x, lambda j: iog.at[i], lambda j: iog.at[j], lambda n: iog.at[pl.ds(0, n)])
 
     lift = (
         lax.broadcasted_iota(jnp.int32, (4, 256), 0)
@@ -375,39 +381,31 @@
 
     kvw_slot = 2 * y + t
 
-    def kvw_copy(j):
-        return remote(kvw_src(j), kvw.at[kvw_slot], "kvw", j, kvw_slot, dev(4 * j + x, z))
+    def kvw_copy(j, stage):
+        return remote(kvw_src(j), kvw.at[kvw_slot], stage, dev(4 * j + x, z), "kvw")
 
     def kvw_send(k, _):
-        kvw_copy(lax.rem(g + k, 8)).start()
+        kvw_copy(lax.rem(g + k, 8), "kvw").start()
         return 0
 
     lax.fori_loop(1, 8, kvw_send, 0)
 
     @pl.when(t == z)
     def _():
-        local(kvw_src(g), kvw.at[kvw_slot], "kvw", kvw_slot).start()
+        local(kvw_src(g), kvw.at[kvw_slot], "kvw").start()
 
     @pl.when(t != z)
     def _():
-        kvw_copy(g).start()
-
-    def kvw_received(k, _):
-        local(kvw.at[k], kvw.at[k], "kvw", k).wait()
-        return 0
-
-    def kvw_sent(k, _):
-        kvw_copy(lax.rem(g + k, 8)).wait_send()
-        return 0
+        kvw_copy(g, "kvx").start()
 
     def kvw_finish():
-        lax.fori_loop(1, 8, kvw_sent, 0)
+        all_sent(kvw.at[pl.ds(0, 7)], "kvw")
 
         @pl.when(t != z)
         def _():
-            kvw_copy(g).wait_send()
-
-    pending["kvw"] = lambda: lax.fori_loop(0, 8, kvw_received, 0)
+            kvw_copy(g, "kvx").wait_send()
+
+    pending["kvw"] = local(kvw, kvw, "kvw").wait
     finish.append(kvw_finish)
     io_all = jnp.concatenate([iog[j].astype(F32) for j in range(8)], axis=0)
     in_vec = io_all[:, :256]
@@ -441,13 +439,13 @@
     gm[:, own_rows] = (gated * mix_gain[...]).astype(BF16)
     swap("gm", gm.at[:, own_rows], gm.at[:, own_rows], sibling)
     sq[i] = row_sums(gated)
-    exchange("sq", 8, i, dev_big_x, lambda j: sq.at[i], lambda j: sq.at[j])
+    exchange("sq", 8, i, dev_big_x, lambda j: sq.at[i], lambda j: sq.at[j], lambda n: sq.at[pl.ds(0, n)])
     arrive("sq")
     group_sum = sq[0]
     for j in range(1, 8):
         group_sum = group_sum + sq[j]
     inverse = to_column(lax.rsqrt(group_sum * (1.0 / 2048.0) + 1e-05))
-    arrive(("gm", 0), ("loc", 1), ("w", 0))
+    arrive("gm", "loc1", "w0")
 
     my_rows = pl.ds(al(48 * y, 48), 48)
     low = pl.ds(0, 256)
@@ -480,6 +478,7 @@
                 dev_y,
                 lambda j, c=c: p.at[c, :, rows_of(j), low],
                 lambda j, c=c: a1.at[c, j],
+                lambda n, c=c: a1.at[c, pl.ds(0, n)],
             )
             exchange(
                 nb1 + tails[c],
@@ -488,6 +487,7 @@
                 dev_x,
                 lambda j, c=c: p.at[c, j, :, high],
                 lambda j, c=c: b1.at[c, j],
+                lambda n, c=c: b1.at[c, pl.ds(0, n)],
             )
         for c in range(2):
             arrive(na1 + tails[c])
@@ -503,6 +503,7 @@
                 dev_x,
                 lambda j, c=c: sa.at[c, j],
                 lambda j, c=c: a2.at[c, j],
+                lambda n, c=c: a2.at[c, pl.ds(0, n)],
             )
             arrive(nb1 + tails[c])
             total = p[c, x, :, 256:512].astype(F32)
@@ -516,6 +517,7 @@
                 dev_y,
                 lambda j, c=c: sb.at[c, rows_of(j)],
                 lambda j, c=c: b2.at[c, j],
+                lambda n, c=c: b2.at[c, pl.ds(0, n)],
             )
         for c in range(2):
             arrive(na2 + tails[c])
@@ -528,9 +530,9 @@
             for k in range(1, 4):
                 total = total + b2[c, lax.rem(y + k, 4)].astype(F32)
             zs[c, :, 256:512] = total.astype(BF16)
-            swap(nz, zs.at[c], zr.at[c], zpeer, c)
+            swap(nz + str(c), zs.at[c], zr.at[c], zpeer)
         for c in range(2):
-            arrive((nz, c))
+            arrive(nz + str(c))
             use(c, zs[c].astype(F32) + zr[c].astype(F32))
 
     feature = al(1024 * (4 * t + x), 1024)
@@ -551,6 +553,7 @@
             dev_x,
             lambda j: mid.at[c, x, my_rows, low],
             lambda j: mid.at[c, j, my_rows, low],
+            lambda n: mid.at[c, pl.ds(0, n), my_rows, low],
         )
         exchange(
             "mb1" + tail,
@@ -559,6 +562,7 @@
             dev_y,
             lambda j: mid.at[c, x, my_rows, high],
             lambda j: mid.at[c, x, rows_of(j), high],
+            lambda n: mid.at[c, x, pl.ds(0, 48 * n), high],
         )
         squares.append(row_sums(residual))
 
@@ -579,7 +583,7 @@
         use_mix,
     )
     sq2[i] = squares[0] + squares[1]
-    exchange("sq2", 8, i, dev_big_x, lambda j: sq2.at[i], lambda j: sq2.at[j])
+    exchange("sq2", 8, i, dev_big_x, lambda j: sq2.at[i], lambda j: sq2.at[j], lambda n: sq2.at[pl.ds(0, n)])
     for c in range(2):
         tail = ("", "x")[c]
         arrive("ma1" + tail)
@@ -590,6 +594,7 @@
             dev_y,
             lambda j, c=c: mid.at[c, :, my_rows, low],
             lambda j, c=c: mid.at[c, :, rows_of(j), low],
+            lambda n, c=c: mid.at[c, :, pl.ds(0, 48 * n), low],
         )
         arrive("mb1" + tail)
         exchange(
@@ -599,19 +604,20 @@
             dev_x,
             lambda j, c=c: mid.at[c, x, :, high],
             lambda j, c=c: mid.at[c, j, :, high],
+            lambda n, c=c: mid.at[c, pl.ds(0, n), :, high],
         )
     arrive("sq2")
     row_sum = sq2[0]
     for j in range(1, 8):
         row_sum = row_sum + sq2[j]
     sqy[y] = row_sum
-    exchange("sqy", 4, y, dev_y, lambda j: sqy.at[y], lambda j: sqy.at[j])
+    exchange("sqy", 4, y, dev_y, lambda j: sqy.at[y], lambda j: sqy.at[j], lambda n: sqy.at[pl.ds(0, n)])
     arrive("sqy")
     scale = jnp.concatenate(
         [to_column(lax.rsqrt(sqy[j] * (1.0 / 8192.0) + 1e-05)) for j in range(4)], axis=0
     )
 
-    arrive(("loc", 2), ("w", 1), "kvw")
+    arrive("loc2", "w1", "kvw")
     query = jnp.zeros((192, 256), F32)
     pair = jnp.zeros((192, 256), F32)
     for c in range(2):
@@ -634,7 +640,7 @@
     pair = pair * scale
     for j in range(8):
         kvp[j] = pair[24 * j : 24 * j + 24]
-    exchange("kvr", 8, i, dev_big_x, lambda j: kvp.at[j], lambda j: kvr.at[j])
+    exchange("kvr", 8, i, dev_big_x, lambda j: kvp.at[j], lambda j: kvr.at[j], lambda n: kvr.at[pl.ds(0, n)])
     qs[...] = query
     swap("q", qs, qr, sibling)
 
@@ -643,9 +649,9 @@
     for k in range(1, 8):
         pair_sum = pair_sum + kvr[lax.rem(i + k, 8)]
     kvg[i] = pair_sum.astype(BF16)
-    exchange("kva", 8, i, dev_big_x, lambda j: kvg.at[i], lambda j: kvg.at[j])
-
-    arrive(("q", 0))
+    exchange("kva", 8, i, dev_big_x, lambda j: kvg.at[i], lambda j: kvg.at[j], lambda n: kvg.at[pl.ds(0, n)])
+
+    arrive("q")
     query_rows = ((qs[...] + qr[...]) * (scale * (128.0**-0.5))).astype(BF16)
     arrive("ca2")
     query_of = []
@@ -704,9 +710,9 @@
             result = result + weight.astype(BF16).astype(F32) * value
         os[p, :, 0:128] = result
         os[p, :, 128:256] = jnp.where(wide_lane < 64, top, total)
-        swap("at", os.at[p], orr.at[p], sibling, p)
+        swap("at" + str(p), os.at[p], orr.at[p], sibling)
     for p in range(3):
-        arrive(("at", p))
+        arrive("at" + str(p))
         mine_top, mine_total = os[p, :, 128:129], os[p, :, 192:193]
         peer_top, peer_total = orr[p, :, 128:129], orr[p, :, 192:193]
         top = jnp.maximum(mine_top, peer_top)
@@ -720,7 +726,7 @@
                     result[64 * head + 16 * step : 64 * head + 16 * step + 16]
                 )
 
-    arrive(("loc", 3), ("w", 2))
+    arrive("loc3", "w2")
 
     def use_out(c, value):
         value = res[c] + value
@@ -749,9 +755,7 @@
 
     def fin_copy(k):
         target = 16 * y + k
-        return remote(
-            fo.at[k], fi.at[i], "fin", k, i, dev(lax.div(target, 2), lax.rem(target, 2))
-        )
+        return remote(fo.at[k], fi.at[i], "fin", dev(lax.div(target, 2), lax.rem(target, 2)))
 
     @pl.when(sends)
     def _():
@@ -761,7 +765,7 @@
         def send(k, _):
             @pl.when(16 * y + k == me)
             def _():
-                local(fo.at[k], fi.at[i], "fin", i).start()
+                local(fo.at[k], fi.at[i], "fin").start()
 
             @pl.when(16 * y + k != me)
             def _():
@@ -771,23 +775,18 @@
 
         lax.fori_loop(0, 16, send, 0)
 
-    def fin_received(k, _):
-        local(fi.at[k], fi.at[k], "fin", k).wait()
-        return 0
+    keeps = sends & (lax.div(me, 16) == y)
 
     def fin_finish():
-        @pl.when(sends)
+        @pl.when(keeps)
         def _():
-            def sent(k, _):
-                @pl.when(16 * y + k != me)
-                def _():
-                    fin_copy(k).wait_send()
-
-                return 0
-
-            lax.fori_loop(0, 16, sent, 0)
-
-    lax.fori_loop(0, 8, fin_received, 0)
+            all_sent(fo.at[pl.ds(0, 15)], "fin")
+
+        @pl.when(sends & (lax.div(me, 16) != y))
+        def _():
+            all_sent(fo, "fin")
+
+    local(fi, fi, "fin").wait()
     finish.append(fin_finish)
     for j in range(8):
         place_j = 1024 * (4 * (j % 2) + j // 2)
@@ -852,8 +851,9 @@
         v((56, 1024), F32),
         v((16, 8, 1024)),
         v((8, 8, 1024)),
-        pltpu.SemaphoreType.DMA((len(STAGES), 16)),
-        pltpu.SemaphoreType.DMA((len(STAGES), 16)),
+        pltpu.SemaphoreType.DMA((len(STAGES),)),
+        pltpu.SemaphoreType.DMA((len(STAGES),)),
+        pltpu.SemaphoreType.DMA((8,)),
     ]
 
 

time: 138 us -> 123 us (0.89)
  Pallas kernels: 132 us -> 117 us
    pallas_call x1, Pallas kernels: 132 us -> 117 us  [shards(): pl.pallas_call(kernel, out_shape=jax.ShapeDtypeStruct((3, 8192), BF16), i...]
where the time goes in v2:
time: 123 us
  Pallas kernels  117 us (95%)
  local copies, waits for them, and re-layouts  5.83 us (5%)
    pallas_call x1, Pallas kernels, shards(): pl.pallas_call(kernel, out_shape=jax.ShapeDtypeStruct((3, 8192), BF16), i...  117 us
    unnamed x6, local copies, waits for them, and re-layouts  3.87 us

profile of v2, /device:TPU:1, one launch (start us, length us, event | category | flops | bytes accessed | tf_op | source)
XLA Modules:
  0.0 122.9 jit_solution(9568967822216886527)
XLA Ops:
  0.0 0.0 copy-start
  0.0 1.3 %copy.32 = bf16[3,256,64,4]{1,2,3,0:T(8,128)(2,1)S(1)} copy(f32[3,256,64,4]{1,3,2,0:T(4,128)} %param.20) | data formatting | bytes 1179648 | tf_op args[2]
  1.3 0.4 copy.29
  1.7 0.2 pad.4.clone
  1.9 0.7 reshape.12
  2.6 1.1 copy.28.st_h
  3.6 0.0 copy-done
  3.7 0.7 copy.33
  4.4 117.0 %shard_map.172 = bf16[3,8192]{1,0:T(4,128)(2,1)} custom-call(s32[3]{0:T(128)} %lens.1, bf16[192,8192]{1,0:T(8,128)(2,1)} %bitcast.17, bf16[8,8,16,256]{3,2,1,0:T(8,128)(2,1)} %copy.28.st_h, bf16[8,3,16,256]{3,2,1,0:T(8,128)(2,1)} %bitcast.18, f32[1,8192]{1,0:T(1,128)} %bitcast.20, bf16[8192,256]{1,0:T(8,128)(2,1)} %wg_h.1, bf16[8192,256]{1,0:T(8,128)(2,1)} %wi_h.1, ...), custom_call_target="tpu_custom_call" | custom-call | flops 4000000000 | bytes 24000000 | tf_op jit(solution)/shard_map/pallas_call | solution.py:887
  121.4 1.5 %copy.35 = bf16[3,8192]{1,0:T(4,128)(2,1)} copy(bf16[3,8192]{1,0:T(4,128)(2,1)} %shard_map.172) | data formatting | bytes 98304
Async XLA Ops:
  0.0 3.7 %copy-start = (bf16[3,16,8,256]{3,2,1,0:T(8,128)(2,1)S(1)}, bf16[3,16,8,256]{3,2,1,0:T(8,128)(2,1)}, u32[]{:S(2)}) copy-start(bf16[3,16,8,256]{3,2,1,0:T(8,128)(2,1)} %param.21) | copy-start | bytes 589828

commit v3 on v2

--- a/solution.py
+++ b/solution.py
@@ -59,6 +59,44 @@
     "loc1",
     "loc2",
     "loc3",
+    "loc4",
+    "a1r",
+    "a1d",
+    "a1c",
+    "a1xr",
+    "a1xd",
+    "a1xc",
+    "b1r",
+    "b1d",
+    "b1c",
+    "b1xr",
+    "b1xd",
+    "b1xc",
+    "c1r",
+    "c1d",
+    "c1c",
+    "c1xr",
+    "c1xd",
+    "c1xc",
+    "d1r",
+    "d1d",
+    "d1c",
+    "d1xr",
+    "d1xd",
+    "d1xc",
+    "ma2f",
+    "ma2g",
+    "ma2o",
+    "ma2xf",
+    "ma2xg",
+    "ma2xo",
+    "mb2f",
+    "mb2g",
+    "mb2o",
+    "mb2xf",
+    "mb2xg",
+    "mb2xo",
+    "loc5",
     "rz0",
     "rz1",
     "sz0",
@@ -136,6 +174,8 @@
     part,
     ra1,
     rb1,
+    rja,
+    rjb,
     qa,
     qb,
     ra2,
@@ -158,6 +198,8 @@
     part2,
     rc1,
     rd1,
+    rjc,
+    rjd,
     qc,
     qd,
     rc2,
@@ -167,6 +209,13 @@
     fin,
     fo,
     fi,
+    plain,
+    sraw,
+    stage,
+    stw,
+    craw,
+    cwide,
+    cw,
     ssem,
     rsem,
     psem,
@@ -239,6 +288,50 @@
         pending[stage] = copy.wait_recv
         finish.append(copy.wait_send)
 
+    def ring_start(stage, me, device, half, buf):
+        right, left, far = (lax.rem(me + k, 4) for k in (1, 3, 2))
+        remote(half(far, 0), buf.at[0], stage, device(right), stage + "r").start()
+        remote(half(far, 1), buf.at[1], stage, device(left), stage + "r").start()
+        remote(half(right, 1), buf.at[2], stage, device(right), stage + "d").start()
+        remote(half(left, 0), buf.at[3], stage, device(left), stage + "d").start()
+        for n, part_name in enumerate("rdc"):
+            landed = buf.at[pl.ds(2 * n, 2)]
+            pending[stage + part_name] = local(landed, landed, stage + part_name).wait
+
+    def ring_pass(stage, me, device, half, buf, joined):
+        right, left = lax.rem(me + 1, 4), lax.rem(me + 3, 4)
+        arrive(stage + "r")
+        joined[0] = (half(right, 0)[...].astype(F32) + buf[0].astype(F32)).astype(BF16)
+        remote(joined.at[0], buf.at[4], stage, device(right), stage + "c").start()
+        joined[1] = (half(left, 1)[...].astype(F32) + buf[1].astype(F32)).astype(BF16)
+        remote(joined.at[1], buf.at[5], stage, device(left), stage + "c").start()
+        finish.append(lambda: all_sent(buf, stage))
+
+    def ring_total(stage, me, half, buf):
+        arrive(stage + "d", stage + "c")
+        return [
+            half(me, h)[...].astype(F32) + buf[3 - h].astype(F32) + buf[4 + h].astype(F32)
+            for h in range(2)
+        ]
+
+    def spread_start(stage, me, device, half):
+        right, left = device(lax.rem(me + 1, 4)), device(lax.rem(me + 3, 4))
+        remote(half(me, 0), half(me, 0), stage, right, stage + "f").start()
+        remote(half(me, 1), half(me, 1), stage, left, stage + "f").start()
+        remote(half(me, 1), half(me, 1), stage, right, stage + "g").start()
+        remote(half(me, 0), half(me, 0), stage, left, stage + "g").start()
+
+    def spread_pass(stage, me, device, half, span):
+        right, left = lax.rem(me + 1, 4), lax.rem(me + 3, 4)
+        one = span(1)
+        local(one, one, stage + "f").wait()
+        remote(half(left, 0), half(left, 0), stage, device(right), stage + "o").start()
+        remote(half(right, 1), half(right, 1), stage, device(left), stage + "o").start()
+        pending[stage + "g"] = local(one, one, stage + "g").wait
+        pending[stage + "o"] = local(one, one, stage + "o").wait
+        everything = span(3)
+        finish.append(lambda: all_sent(everything, stage))
+
     def fetch(stage, src, dst):
         copy = local(src, dst, stage)
         copy.start()
@@ -254,6 +347,8 @@
         for wait in finish:
             wait()
 
+    fetch("loc4", cache_h, craw)
+    fetch("loc5", st_h, sraw)
     fetch("loc0", hid_h, hid)
 
     def proj_copy(c, src, dst, slot):
@@ -285,13 +380,21 @@
         return 0
 
     lax.fori_loop(1, 64, greet, 0)
+    arrive("loc4")
+    cache_rows = craw[...].astype(F32).reshape(384, 256)
+    for side in range(2):
+        lanes = slice(128 * side, 128 * side + 128)
+        cwide[side] = cache_rows[:, lanes]
+        for j in range(8):
+            picked = cwide[side, pl.ds(j, 48, stride=8), :]
+            cw[j, :, :, lanes] = picked.astype(BF16).reshape(3, 16, 128)
+
     pl.semaphore_wait(barrier, 63)
 
     def wio_src(j):
         return wio_h.at[:, pl.ds(al(512 * j, 512), 512)]
 
-    exchange("ca1", 8, g, dev_big_y, lambda j: cache_h.at[j], lambda j: ca1.at[:, j], lambda n: ca1.at[:, pl.ds(0, n)], own=True)
-    exchange("st1", 8, i, dev_big_x, lambda j: st_h.at[j], lambda j: st1.at[j], lambda n: st1.at[pl.ds(0, n)], own=True)
+    exchange("ca1", 8, g, dev_big_y, lambda j: cw.at[j], lambda j: ca1.at[:, j], lambda n: ca1.at[:, pl.ds(0, n)], own=True)
     exchange("wio", 8, g, dev_big_y, wio_src, lambda j: wio.at[j], lambda n: wio.at[pl.ds(0, n)], own=True)
 
     half = al(4096 * t, 4096)
@@ -305,6 +408,26 @@
     fetch("loc3", wo_h.at[:, pl.ds(half, 4096)], wo.at[head_rows])
     swap("w2", wo_h.at[:, pl.ds(other, 4096)], wo.at[head_rows], sibling)
 
+    stage[...] = jnp.zeros_like(stage)
+    line = lax.broadcasted_iota(jnp.int32, (256, 256), 0)
+    block_of = lax.rem(line, 64)
+    head_of = 32 * lax.rem(block_of, 8) + 4 * lax.div(block_of, 8) + lax.div(line, 64)
+    pick_head = (head_of == lax.broadcasted_iota(jnp.int32, (256, 256), 1)).astype(F32).astype(BF16)
+    arrive("loc5")
+    for p in range(3):
+        for n in range(4):
+            turned = nt_dot(pick_head, sraw[p, :, n, :].astype(BF16))
+            for side in range(2):
+                stage[side, pl.ds(4 * p + n, 64, stride=16), :] = jnp.concatenate(
+                    [turned[128 * side : 128 * side + 64], turned[128 * side + 64 : 128 * side + 128]],
+                    axis=1,
+                )
+    for side in range(2):
+        stw[:, :, :, 128 * side : 128 * side + 128] = (
+            stage[side].astype(BF16).reshape(8, 8, 16, 128)
+        )
+    exchange("st1", 8, i, dev_big_x, lambda j: stw.at[j], lambda j: st1.at[j], lambda n: st1.at[pl.ds(0, n)], own=True)
+
     arrive("loc0")
 
     def norm_rows(r, _):
@@ -347,9 +470,9 @@
         iop[j] = io_part[24 * j : 24 * j + 24]
     exchange("iors", 8, i, dev_big_x, lambda j: iop.at[j], lambda j: ior.at[j], lambda n: ior.at[pl.ds(0, n)])
     arrive("iors")
-    io_sum = iop[i]
+    io_sum = iop[i].astype(F32)
     for k in range(1, 8):
-        io_sum = io_sum + ior[lax.rem(i + k, 8)]
+        io_sum = io_sum + ior[lax.rem(i + k, 8)].astype(F32)
     iog[i] = io_sum.astype(BF16)
     exchange("ioag", 8, i, dev_big_x, lambda j: iog.at[i], lambda j: iog.at[j], lambda n: iog.at[pl.ds(0, n)])
 
@@ -440,11 +563,13 @@
     swap("gm", gm.at[:, own_rows], gm.at[:, own_rows], sibling)
     sq[i] = row_sums(gated)
     exchange("sq", 8, i, dev_big_x, lambda j: sq.at[i], lambda j: sq.at[j], lambda n: sq.at[pl.ds(0, n)])
-    arrive("sq")
-    group_sum = sq[0]
-    for j in range(1, 8):
-        group_sum = group_sum + sq[j]
-    inverse = to_column(lax.rsqrt(group_sum * (1.0 / 2048.0) + 1e-05))
+    def mix_scale():
+        arrive("sq")
+        group_sum = sq[0]
+        for j in range(1, 8):
+            group_sum = group_sum + sq[j]
+        return to_column(lax.rsqrt(group_sum * (1.0 / 2048.0) + 1e-05))
+
     arrive("gm", "loc1", "w0")
 
     my_rows = pl.ds(al(48 * y, 48), 48)
@@ -454,9 +579,16 @@
     def rows_of(j):
         return pl.ds(al(48 * j, 48), 48)
 
-    def reduce_scatter(names, left, weight, column, p, a1, b1, sa, sb, a2, b2, zs, zr, use):
+    def half_a(p, c):
+        return lambda j, h: p.at[c, pl.ds(2 * h, 2), rows_of(j), low]
+
+    def half_b(p, c):
+        return lambda j, h: p.at[c, j, pl.ds(96 * h, 96), high]
+
+    def reduce_scatter(names, left, weight, scaling, p, a1, b1, ja, jb, sa, sb, a2, b2, zs, zr, use):
         na1, nb1, na2, nb2, nz = names
         tails = ("", "x")
+        scales = []
 
         for c in range(2):
 
@@ -465,37 +597,34 @@
                 hh = lax.rem(n, 2)
                 cols = pl.ds(al(1024 * xx + 512 * hh + 256 * c, 256), 256)
                 value = jnp.dot(left[...], weight[:, cols], preferred_element_type=F32)
-                if column is not None:
-                    value = value * column
+                if scaling is not None and c == 0:
+                    plain[n] = value
+                    return 0
+                if scaling is not None:
+                    value = value * scales[0]
                 p[c, xx, :, pl.ds(al(256 * hh, 256), 256)] = value.astype(BF16)
                 return 0
 
-            lax.fori_loop(0, 8, block, 0)
-            exchange(
-                na1 + tails[c],
-                4,
-                y,
-                dev_y,
-                lambda j, c=c: p.at[c, :, rows_of(j), low],
-                lambda j, c=c: a1.at[c, j],
-                lambda n, c=c: a1.at[c, pl.ds(0, n)],
-            )
-            exchange(
-                nb1 + tails[c],
-                4,
-                x,
-                dev_x,
-                lambda j, c=c: p.at[c, j, :, high],
-                lambda j, c=c: b1.at[c, j],
-                lambda n, c=c: b1.at[c, pl.ds(0, n)],
-            )
+            lax.fori_loop(0, 8, block, 0, unroll=4)
+            if scaling is not None and c == 0:
+                scales.append(scaling())
+
+                def rescale(n, _):
+                    p[0, lax.div(n, 2), :, pl.ds(al(256 * lax.rem(n, 2), 256), 256)] = (
+                        plain[n] * scales[0]
+                    ).astype(BF16)
+                    return 0
+
+                lax.fori_loop(0, 8, rescale, 0)
+            ring_start(na1 + tails[c], y, dev_y, half_a(p, c), a1.at[c])
+            ring_start(nb1 + tails[c], x, dev_x, half_b(p, c), b1.at[c])
         for c in range(2):
-            arrive(na1 + tails[c])
-            for xx in range(4):
-                total = p[c, xx, my_rows, 0:256].astype(F32)
-                for k in range(1, 4):
-                    total = total + a1[c, lax.rem(y + k, 4), xx].astype(F32)
-                sa[c, xx] = total.astype(BF16)
+            ring_pass(na1 + tails[c], y, dev_y, half_a(p, c), a1.at[c], ja.at[c])
+            ring_pass(nb1 + tails[c], x, dev_x, half_b(p, c), b1.at[c], jb.at[c])
+        for c in range(2):
+            totals = ring_total(na1 + tails[c], y, half_a(p, c), a1.at[c])
+            for h in range(2):
+                sa[c, 2 * h : 2 * h + 2] = totals[h].astype(BF16)
             exchange(
                 na2 + tails[c],
                 4,
@@ -505,11 +634,9 @@
                 lambda j, c=c: a2.at[c, j],
                 lambda n, c=c: a2.at[c, pl.ds(0, n)],
             )
-            arrive(nb1 + tails[c])
-            total = p[c, x, :, 256:512].astype(F32)
-            for k in range(1, 4):
-                total = total + b1[c, lax.rem(x + k, 4)].astype(F32)
-            sb[c] = total.astype(BF16)
+            totals = ring_total(nb1 + tails[c], x, half_b(p, c), b1.at[c])
+            for h in range(2):
+                sb[c, 96 * h : 96 * h + 96, :] = totals[h].astype(BF16)
             exchange(
                 nb2 + tails[c],
                 4,
@@ -570,10 +697,12 @@
         ("a1", "b1", "a2", "b2", "rz"),
         gm,
         wm,
-        inverse,
+        mix_scale,
         part,
         ra1,
         rb1,
+        rja,
+        rjb,
         qa,
         qb,
         ra2,
@@ -587,24 +716,20 @@
     for c in range(2):
         tail = ("", "x")[c]
         arrive("ma1" + tail)
-        exchange(
+        spread_start("ma2" + tail, y, dev_y, half_a(mid, c))
+        arrive("mb1" + tail)
+        spread_start("mb2" + tail, x, dev_x, half_b(mid, c))
+    for c in range(2):
+        tail = ("", "x")[c]
+        spread_pass(
             "ma2" + tail,
-            4,
             y,
             dev_y,
-            lambda j, c=c: mid.at[c, :, my_rows, low],
-            lambda j, c=c: mid.at[c, :, rows_of(j), low],
+            half_a(mid, c),
             lambda n, c=c: mid.at[c, :, pl.ds(0, 48 * n), low],
         )
-        arrive("mb1" + tail)
-        exchange(
-            "mb2" + tail,
-            4,
-            x,
-            dev_x,
-            lambda j, c=c: mid.at[c, x, :, high],
-            lambda j, c=c: mid.at[c, j, :, high],
-            lambda n, c=c: mid.at[c, pl.ds(0, n), :, high],
+        spread_pass(
+            "mb2" + tail, x, dev_x, half_b(mid, c), lambda n, c=c: mid.at[c, pl.ds(0, n), :, high]
         )
     arrive("sq2")
     row_sum = sq2[0]
@@ -622,7 +747,8 @@
     pair = jnp.zeros((192, 256), F32)
     for c in range(2):
         tail = ("", "x")[c]
-        arrive("ma2" + tail, "mb2" + tail)
+        for name in ("ma2", "mb2"):
+            arrive(name + tail + "g", name + tail + "o")
         for xx in range(4):
             for hh in range(2):
                 place = 1024 * xx + 512 * hh + 256 * c
@@ -645,9 +771,9 @@
     swap("q", qs, qr, sibling)
 
     arrive("kvr")
-    pair_sum = kvp[i]
+    pair_sum = kvp[i].astype(F32)
     for k in range(1, 8):
-        pair_sum = pair_sum + kvr[lax.rem(i + k, 8)]
+        pair_sum = pair_sum + kvr[lax.rem(i + k, 8)].astype(F32)
     kvg[i] = pair_sum.astype(BF16)
     exchange("kva", 8, i, dev_big_x, lambda j: kvg.at[i], lambda j: kvg.at[j], lambda n: kvg.at[pl.ds(0, n)])
 
@@ -741,6 +867,8 @@
         part2,
         rc1,
         rd1,
+        rjc,
+        rjd,
         qc,
         qd,
         rc2,
@@ -799,8 +927,10 @@
         return pltpu.VMEM(shape, dtype)
 
     reduce_bufs = [
-        v((2, 4, 4, 48, 256)),
-        v((2, 4, 192, 256)),
+        v((2, 6, 2, 48, 256)),
+        v((2, 6, 96, 256)),
+        v((2, 2, 2, 48, 256)),
+        v((2, 2, 96, 256)),
         v((2, 4, 48, 256)),
         v((2, 192, 256)),
         v((2, 4, 48, 256)),
@@ -851,6 +981,13 @@
         v((56, 1024), F32),
         v((16, 8, 1024)),
         v((8, 8, 1024)),
+        v((8, 192, 256), F32),
+        v((3, 64, 4, 256), F32),
+        v((2, 1024, 128), F32),
+        v((8, 8, 16, 256)),
+        v((3, 16, 8, 256)),
+        v((2, 384, 128), F32),
+        v((8, 3, 16, 256)),
         pltpu.SemaphoreType.DMA((len(STAGES),)),
         pltpu.SemaphoreType.DMA((len(STAGES),)),
         pltpu.SemaphoreType.DMA((8,)),
@@ -878,9 +1015,7 @@
     output_weight,
 ):
     hidden = hidden_input.reshape(192, 8192)
-    states = jnp.pad(prompt_states.astype(BF16), ((0, 1), (0, 0), (0, 0), (0, 0)))
-    states = states.reshape(4, 8, 8, 4, 64, 4).transpose(2, 1, 0, 5, 3, 4).reshape(8, 8, 16, 256)
-    cache = prompt_cache.transpose(2, 0, 1, 3)
+    states = prompt_states.transpose(0, 2, 3, 1)
     vmem = pl.BlockSpec(memory_space=pltpu.VMEM)
     smem = pl.BlockSpec(memory_space=pltpu.SMEM)
     anyw = pl.BlockSpec(memory_space=pl.ANY)
@@ -919,7 +1054,7 @@
         prompt_lengths,
         hidden,
         states,
-        cache,
+        prompt_cache,
         input_gain[None, :],
         gate_weight,
         input_weight,

time: 123 us -> 114 us (0.927)
  local copies, waits for them, and re-layouts: 5.83 us -> 1.49 us
  Pallas kernels: 117 us -> 113 us
    pallas_call x1, Pallas kernels: 117 us -> 113 us  [shards(): pl.pallas_call(kernel, out_shape=jax.ShapeDtypeStruct((3, 8192), BF16), i...]
    unnamed x6 -> x1, local copies, waits for them, and re-layouts: 3.87 us -> 1.49 us
    reshape x2 -> x0, local copies, waits for them, and re-layouts: 1.74 us -> none  [shards(): states.reshape(4, 8, 8, 4, 64, 4).transpose(2, 1, 0, 5, 3, 4)]
where the time goes in v3:
time: 114 us
  Pallas kernels  113 us (99%)
  local copies, waits for them, and re-layouts  1.49 us (1%)
    pallas_call x1, Pallas kernels, shards(): pl.pallas_call(kernel, out_shape=jax.ShapeDtypeStruct((3, 8192), BF16), i...  113 us

profile of v3, /device:TPU:1, one launch (start us, length us, event | category | flops | bytes accessed | tf_op | source)
XLA Modules:
  0.0 114.2 jit_solution(11217050443471409298)
XLA Ops:
  0.0 112.7 %shard_map.172 = bf16[3,8192]{1,0:T(4,128)(2,1)} custom-call(s32[3]{0:T(128)} %lens.1, bf16[192,8192]{1,0:T(8,128)(2,1)} %bitcast.9, f32[3,64,4,256]{3,2,1,0:T(4,128)} %bitcast.10, bf16[3,16,8,256]{3,2,1,0:T(8,128)(2,1)} %cache_h.1, f32[1,8192]{1,0:T(1,128)} %bitcast.12, bf16[8192,256]{1,0:T(8,128)(2,1)} %wg_h.1, bf16[8192,256]{1,0:T(8,128)(2,1)} %wi_h.1, ...), custom_call_target="tpu_custom_call" | custom-call | flops 4000000000 | bytes 24000000 | tf_op jit(solution)/shard_map/pallas_call | solution.py:1022
  112.7 1.5 %copy.20 = bf16[3,8192]{1,0:T(4,128)(2,1)} copy(bf16[3,8192]{1,0:T(4,128)(2,1)} %shard_map.172) | data formatting | bytes 98304

commit v4 on v3

--- a/solution.py
+++ b/solution.py
@@ -10,103 +10,7 @@
 MESH = pl.DeviceIdType.MESH
 HIGH = lax.Precision.HIGHEST
 
-STAGES = (
-    "wio",
-    "st1",
-    "kvw",
-    "kvx",
-    "ca1",
-    "st2",
-    "ca2",
-    "iors",
-    "ioag",
-    "sq",
-    "gm",
-    "a1",
-    "b1",
-    "a2",
-    "b2",
-    "sq2",
-    "sqy",
-    "ma1",
-    "mb1",
-    "ma2",
-    "mb2",
-    "q",
-    "kvr",
-    "kva",
-    "c1",
-    "d1",
-    "c2",
-    "d2",
-    "fin",
-    "a1x",
-    "b1x",
-    "a2x",
-    "b2x",
-    "ma1x",
-    "mb1x",
-    "ma2x",
-    "mb2x",
-    "c1x",
-    "d1x",
-    "c2x",
-    "d2x",
-    "w0",
-    "w1",
-    "w2",
-    "loc0",
-    "loc1",
-    "loc2",
-    "loc3",
-    "loc4",
-    "a1r",
-    "a1d",
-    "a1c",
-    "a1xr",
-    "a1xd",
-    "a1xc",
-    "b1r",
-    "b1d",
-    "b1c",
-    "b1xr",
-    "b1xd",
-    "b1xc",
-    "c1r",
-    "c1d",
-    "c1c",
-    "c1xr",
-    "c1xd",
-    "c1xc",
-    "d1r",
-    "d1d",
-    "d1c",
-    "d1xr",
-    "d1xd",
-    "d1xc",
-    "ma2f",
-    "ma2g",
-    "ma2o",
-    "ma2xf",
-    "ma2xg",
-    "ma2xo",
-    "mb2f",
-    "mb2g",
-    "mb2o",
-    "mb2xf",
-    "mb2xg",
-    "mb2xo",
-    "loc5",
-    "rz0",
-    "rz1",
-    "sz0",
-    "sz1",
-    "at0",
-    "at1",
-    "at2",
-    "pro",
-)
-STAGE = {name: number for number, name in enumerate(STAGES)}
+SENDS, LANDINGS = 51, 80
 
 
 def nt_dot(left, right, precision=None):
@@ -249,21 +153,26 @@
     sibling = dev(s, 1 - t)
     zpeer = dev(16 * (1 - z) + 4 * y + x, t)
 
+    sends_of, landings_of = {}, {}
+
+    def number(table, stage):
+        return table.setdefault(stage, len(table))
+
     def remote(src, dst, stage, device, landing=None):
         return pltpu.make_async_remote_copy(
             src_ref=src,
             dst_ref=dst,
-            send_sem=ssem.at[STAGE[stage]],
-            recv_sem=rsem.at[STAGE[landing or stage]],
+            send_sem=ssem.at[number(sends_of, stage)],
+            recv_sem=rsem.at[number(landings_of, landing or stage)],
             device_id=device,
             device_id_type=MESH,
         )
 
     def local(src, dst, stage):
-        return pltpu.make_async_copy(src, dst, rsem.at[STAGE[stage]])
+        return pltpu.make_async_copy(src, dst, rsem.at[number(landings_of, stage)])
 
     def all_sent(ref, stage):
-        pltpu.make_async_copy(ref, ref, ssem.at[STAGE[stage]]).wait()
+        pltpu.make_async_copy(ref, ref, ssem.at[number(sends_of, stage)]).wait()
 
     pending = {}
     finish = []
@@ -464,11 +373,11 @@
 
     lax.fori_loop(0, 8, pick, 0)
     arrive("wio", "st1")
-    exchange("st2", 8, g, dev_big_y, lambda j: st1.at[:, j], lambda j: st2.at[j], lambda n: st2.at[pl.ds(0, n)], own=True)
     io_part = jnp.dot(nio[...], wio[...].reshape(1024, 512), preferred_element_type=F32)
     for j in range(8):
         iop[j] = io_part[24 * j : 24 * j + 24]
     exchange("iors", 8, i, dev_big_x, lambda j: iop.at[j], lambda j: ior.at[j], lambda n: ior.at[pl.ds(0, n)])
+    exchange("st2", 8, g, dev_big_y, lambda j: st1.at[:, j], lambda j: st2.at[j], lambda n: st2.at[pl.ds(0, n)], own=True)
     arrive("iors")
     io_sum = iop[i].astype(F32)
     for k in range(1, 8):
@@ -592,32 +501,32 @@
 
         for c in range(2):
 
-            def block(n, _, c=c):
-                xx = lax.div(n, 2)
-                hh = lax.rem(n, 2)
-                cols = pl.ds(al(1024 * xx + 512 * hh + 256 * c, 256), 256)
-                value = jnp.dot(left[...], weight[:, cols], preferred_element_type=F32)
-                if scaling is not None and c == 0:
-                    plain[n] = value
+            for hh in (1, 0):
+
+                def block(xx, _, c=c, hh=hh):
+                    cols = pl.ds(al(1024 * xx + 512 * hh + 256 * c, 256), 256)
+                    value = jnp.dot(left[...], weight[:, cols], preferred_element_type=F32)
+                    if scaling is not None and c == 0 and hh == 1:
+                        plain[xx] = value
+                        return 0
+                    if scaling is not None:
+                        value = value * scales[0]
+                    p[c, xx, :, 256 * hh : 256 * hh + 256] = value.astype(BF16)
                     return 0
-                if scaling is not None:
-                    value = value * scales[0]
-                p[c, xx, :, pl.ds(al(256 * hh, 256), 256)] = value.astype(BF16)
-                return 0
-
-            lax.fori_loop(0, 8, block, 0, unroll=4)
-            if scaling is not None and c == 0:
-                scales.append(scaling())
-
-                def rescale(n, _):
-                    p[0, lax.div(n, 2), :, pl.ds(al(256 * lax.rem(n, 2), 256), 256)] = (
-                        plain[n] * scales[0]
-                    ).astype(BF16)
-                    return 0
-
-                lax.fori_loop(0, 8, rescale, 0)
-            ring_start(na1 + tails[c], y, dev_y, half_a(p, c), a1.at[c])
-            ring_start(nb1 + tails[c], x, dev_x, half_b(p, c), b1.at[c])
+
+                lax.fori_loop(0, 4, block, 0, unroll=4)
+                if scaling is not None and c == 0 and hh == 1:
+                    scales.append(scaling())
+
+                    def rescale(xx, _):
+                        p[0, xx, :, 256:512] = (plain[xx] * scales[0]).astype(BF16)
+                        return 0
+
+                    lax.fori_loop(0, 4, rescale, 0)
+                if hh == 1:
+                    ring_start(nb1 + tails[c], x, dev_x, half_b(p, c), b1.at[c])
+                else:
+                    ring_start(na1 + tails[c], y, dev_y, half_a(p, c), a1.at[c])
         for c in range(2):
             ring_pass(na1 + tails[c], y, dev_y, half_a(p, c), a1.at[c], ja.at[c])
             ring_pass(nb1 + tails[c], x, dev_x, half_b(p, c), b1.at[c], jb.at[c])
@@ -737,11 +646,6 @@
         row_sum = row_sum + sq2[j]
     sqy[y] = row_sum
     exchange("sqy", 4, y, dev_y, lambda j: sqy.at[y], lambda j: sqy.at[j], lambda n: sqy.at[pl.ds(0, n)])
-    arrive("sqy")
-    scale = jnp.concatenate(
-        [to_column(lax.rsqrt(sqy[j] * (1.0 / 8192.0) + 1e-05)) for j in range(4)], axis=0
-    )
-
     arrive("loc2", "w1", "kvw")
     query = jnp.zeros((192, 256), F32)
     pair = jnp.zeros((192, 256), F32)
@@ -749,6 +653,29 @@
         tail = ("", "x")[c]
         for name in ("ma2", "mb2"):
             arrive(name + tail + "g", name + tail + "o")
+        if c == 1:
+            for xx in range(4):
+                pair = pair + jnp.dot(
+                    mid[lax.rem(x, 2), xx, :, pl.ds(al(256 * lax.div(x, 2), 256), 256)],
+                    kvw[2 * xx : 2 * xx + 2].reshape(256, 256),
+                    preferred_element_type=F32,
+                )
+            arrive("sqy")
+            scale = jnp.concatenate(
+                [to_column(lax.rsqrt(sqy[j] * (1.0 / 8192.0) + 1e-05)) for j in range(4)], axis=0
+            )
+            pair = pair * scale
+            for j in range(8):
+                kvp[j] = pair[24 * j : 24 * j + 24]
+            exchange(
+                "kvr",
+                8,
+                i,
+                dev_big_x,
+                lambda j: kvp.at[j],
+                lambda j: kvr.at[j],
+                lambda n: kvr.at[pl.ds(0, n)],
+            )
         for xx in range(4):
             for hh in range(2):
                 place = 1024 * xx + 512 * hh + 256 * c
@@ -757,16 +684,6 @@
                     wq[place : place + 256, :],
                     preferred_element_type=F32,
                 )
-    for xx in range(4):
-        pair = pair + jnp.dot(
-            mid[lax.rem(x, 2), xx, :, pl.ds(al(256 * lax.div(x, 2), 256), 256)],
-            kvw[2 * xx : 2 * xx + 2].reshape(256, 256),
-            preferred_element_type=F32,
-        )
-    pair = pair * scale
-    for j in range(8):
-        kvp[j] = pair[24 * j : 24 * j + 24]
-    exchange("kvr", 8, i, dev_big_x, lambda j: kvp.at[j], lambda j: kvr.at[j], lambda n: kvr.at[pl.ds(0, n)])
     qs[...] = query
     swap("q", qs, qr, sibling)
 
@@ -981,15 +898,15 @@
         v((56, 1024), F32),
         v((16, 8, 1024)),
         v((8, 8, 1024)),
-        v((8, 192, 256), F32),
+        v((4, 192, 256), F32),
         v((3, 64, 4, 256), F32),
         v((2, 1024, 128), F32),
         v((8, 8, 16, 256)),
         v((3, 16, 8, 256)),
         v((2, 384, 128), F32),
         v((8, 3, 16, 256)),
-        pltpu.SemaphoreType.DMA((len(STAGES),)),
-        pltpu.SemaphoreType.DMA((len(STAGES),)),
+        pltpu.SemaphoreType.DMA((SENDS,)),
+        pltpu.SemaphoreType.DMA((LANDINGS,)),
         pltpu.SemaphoreType.DMA((8,)),
     ]
 

time: 114 us -> 113 us (level)
  no operation moved by 1% of the time
where the time goes in v4:
time: 113 us
  Pallas kernels  112 us (99%)
  local copies, waits for them, and re-layouts  1.49 us (1%)
    pallas_call x1, Pallas kernels, shards(): pl.pallas_call(kernel, out_shape=jax.ShapeDtypeStruct((3, 8192), BF16), i...  112 us

profile of v4, /device:TPU:1, one launch (start us, length us, event | category | flops | bytes accessed | tf_op | source)
XLA Modules:
  0.0 113.2 jit_solution(3263074332248572187)
XLA Ops:
  0.0 111.7 %shard_map.172 = bf16[3,8192]{1,0:T(4,128)(2,1)} custom-call(s32[3]{0:T(128)} %lens.1, bf16[192,8192]{1,0:T(8,128)(2,1)} %bitcast.9, f32[3,64,4,256]{3,2,1,0:T(4,128)} %bitcast.10, bf16[3,16,8,256]{3,2,1,0:T(8,128)(2,1)} %cache_h.1, f32[1,8192]{1,0:T(1,128)} %bitcast.12, bf16[8192,256]{1,0:T(8,128)(2,1)} %wg_h.1, bf16[8192,256]{1,0:T(8,128)(2,1)} %wi_h.1, ...), custom_call_target="tpu_custom_call" | custom-call | flops 4000000000 | bytes 24000000 | tf_op jit(solution)/shard_map/pallas_call | solution.py:939
  111.7 1.5 %copy.20 = bf16[3,8192]{1,0:T(4,128)(2,1)} copy(bf16[3,8192]{1,0:T(4,128)(2,1)} %shard_map.172) | data formatting | bytes 98304

commit v5 on v4

--- a/solution.py
+++ b/solution.py
@@ -337,6 +337,9 @@
         )
     exchange("st1", 8, i, dev_big_x, lambda j: stw.at[j], lambda j: st1.at[j], lambda n: st1.at[pl.ds(0, n)], own=True)
 
+    arrive("ca1")
+    exchange("ca2", 4, x, dev_x, lambda j: ca1, lambda j: ca2.at[j], lambda n: ca2.at[pl.ds(0, n)], own=True)
+
     arrive("loc0")
 
     def norm_rows(r, _):
@@ -347,8 +350,6 @@
         return 0
 
     lax.fori_loop(0, 12, norm_rows, 0)
-    arrive("ca1")
-    exchange("ca2", 4, x, dev_x, lambda j: ca1, lambda j: ca2.at[j], lambda n: ca2.at[pl.ds(0, n)], own=True)
 
     accg[...] = jnp.zeros_like(accg)
     acci[...] = jnp.zeros_like(acci)
@@ -378,6 +379,39 @@
         iop[j] = io_part[24 * j : 24 * j + 24]
     exchange("iors", 8, i, dev_big_x, lambda j: iop.at[j], lambda j: ior.at[j], lambda n: ior.at[pl.ds(0, n)])
     exchange("st2", 8, g, dev_big_y, lambda j: st1.at[:, j], lambda j: st2.at[j], lambda n: st2.at[pl.ds(0, n)], own=True)
+
+    def kvw_src(j):
+        return wkv_h.at[:, pl.ds(al(256 * j, 256), 256)]
+
+    kvw_slot = 2 * y + t
+
+    def kvw_copy(j, stage):
+        return remote(kvw_src(j), kvw.at[kvw_slot], stage, dev(4 * j + x, z), "kvw")
+
+    def kvw_send(k, _):
+        kvw_copy(lax.rem(g + k, 8), "kvw").start()
+        return 0
+
+    lax.fori_loop(1, 8, kvw_send, 0)
+
+    @pl.when(t == z)
+    def _():
+        local(kvw_src(g), kvw.at[kvw_slot], "kvw").start()
+
+    @pl.when(t != z)
+    def _():
+        kvw_copy(g, "kvx").start()
+
+    def kvw_finish():
+        all_sent(kvw.at[pl.ds(0, 7)], "kvw")
+
+        @pl.when(t != z)
+        def _():
+            kvw_copy(g, "kvx").wait_send()
+
+    pending["kvw"] = local(kvw, kvw, "kvw").wait
+    finish.append(kvw_finish)
+
     arrive("iors")
     io_sum = iop[i].astype(F32)
     for k in range(1, 8):
@@ -408,37 +442,6 @@
     spread = jnp.where(spread, 1.0, 0.0).astype(BF16)
 
     arrive("ioag")
-    def kvw_src(j):
-        return wkv_h.at[:, pl.ds(al(256 * j, 256), 256)]
-
-    kvw_slot = 2 * y + t
-
-    def kvw_copy(j, stage):
-        return remote(kvw_src(j), kvw.at[kvw_slot], stage, dev(4 * j + x, z), "kvw")
-
-    def kvw_send(k, _):
-        kvw_copy(lax.rem(g + k, 8), "kvw").start()
-        return 0
-
-    lax.fori_loop(1, 8, kvw_send, 0)
-
-    @pl.when(t == z)
-    def _():
-        local(kvw_src(g), kvw.at[kvw_slot], "kvw").start()
-
-    @pl.when(t != z)
-    def _():
-        kvw_copy(g, "kvx").start()
-
-    def kvw_finish():
-        all_sent(kvw.at[pl.ds(0, 7)], "kvw")
-
-        @pl.when(t != z)
-        def _():
-            kvw_copy(g, "kvx").wait_send()
-
-    pending["kvw"] = local(kvw, kvw, "kvw").wait
-    finish.append(kvw_finish)
     io_all = jnp.concatenate([iog[j].astype(F32) for j in range(8)], axis=0)
     in_vec = io_all[:, :256]
     out_vec = io_all[:, 256:]

time: 113 us -> 113 us (level)
  no operation moved by 1% of the time
where the time goes in v5:
time: 113 us
  Pallas kernels  111 us (98%)
  local copies, waits for them, and re-layouts  1.49 us (1%)
    pallas_call x1, Pallas kernels, shards(): pl.pallas_call(kernel, out_shape=jax.ShapeDtypeStruct((3, 8192), BF16), i...  111 us

profile of v5, /device:TPU:1, one launch (start us, length us, event | category | flops | bytes accessed | tf_op | source)
XLA Modules:
  0.0 112.8 jit_solution(776726018009273444)
XLA Ops:
  0.0 111.3 %shard_map.172 = bf16[3,8192]{1,0:T(4,128)(2,1)} custom-call(s32[3]{0:T(128)} %lens.1, bf16[192,8192]{1,0:T(8,128)(2,1)} %bitcast.9, f32[3,64,4,256]{3,2,1,0:T(4,128)} %bitcast.10, bf16[3,16,8,256]{3,2,1,0:T(8,128)(2,1)} %cache_h.1, f32[1,8192]{1,0:T(1,128)} %bitcast.12, bf16[8192,256]{1,0:T(8,128)(2,1)} %wg_h.1, bf16[8192,256]{1,0:T(8,128)(2,1)} %wi_h.1, ...), custom_call_target="tpu_custom_call" | custom-call | flops 4000000000 | bytes 24000000 | tf_op jit(solution)/shard_map/pallas_call | solution.py:942
  111.3 1.5 %copy.20 = bf16[3,8192]{1,0:T(4,128)(2,1)} copy(bf16[3,8192]{1,0:T(4,128)(2,1)} %shard_map.172) | data formatting | bytes 98304
